TPU v7x, 512 devices: a whole 4x4x16 slice. The times are simulated.
512 devices in a mesh: col: 8 (over y, z_hi), row: 64 (over z_lo, x, core).
Axes of the slice: x: 4, y: 4, z: 16 (z_hi: 2, z_lo: 8; z = z_hi * 8 + z_lo), core: 2. Of those that a mesh axis runs over, the one named last changes fastest.
Arguments:
- tokens: bfloat16 [512, 8192], P('row', 'col'), may hold values from -6 to 6
- grad_out: bfloat16 [512, 8192], P('row', 'col'), may hold values from -6 to 6
- gate_weight: bfloat16 [8192, 16384], P('col', 'row'), may hold values from -0.0625 to 0.0625
- up_weight: bfloat16 [8192, 16384], P('col', 'row'), may hold values from -0.0625 to 0.0625
- down_weight: bfloat16 [16384, 8192], P('row', 'col'), may hold values from -0.046875 to 0.046875
- gate_blocks: int32 [64, 8, 8], P('row', 'col'), may hold values from 0 to 15, as said below
- up_blocks: int32 [64, 8, 8], P('row', 'col'), may hold values from 0 to 15, as said below
- down_blocks: int32 [64, 8, 8], P('row', 'col'), may hold values from 0 to 15, as said below
- block_counts: int32 [64, 8, 3], P('row', 'col'), may hold values from 1 to 8, as said below
Outputs:
- grad_in: float32 [512, 8192], P('row', 'col')
- gate_delta: float32 [64, 8, 8, 128, 128], P('row', 'col')
- up_delta: float32 [64, 8, 8, 128, 128], P('row', 'col')
- down_delta: float32 [64, 8, 8, 128, 128], P('row', 'col')
Inputs may be any that keep to these rules, and one draw needn't show every extreme that they name: `block_counts`: entry k of a device counts its trainable blocks of the gate (k = 0), up (k = 1) and down (k = 2) projection; for each projection some device has exactly 8. `gate_blocks`: A device's first block_counts[..., 0] entries are distinct block numbers in increasing order; the rest are 0. `up_blocks`: A device's first block_counts[..., 1] entries are distinct block numbers in increasing order; the rest are 0. `down_blocks`: A device's first block_counts[..., 2] entries are distinct block numbers in increasing order; the rest are 0.
All inputs are finite; a program needn't handle non-finite values.
Results may differ from a plain program's by a relative error of at most 0.0029.
Values may be sent and summed in bfloat16 or wider, within the bound.
No kernel may reach another device: no remote copies, remote signals or barrier semaphores. Data moves between devices by JAX's collectives and lax.ppermute only.
A program may use at most 64 MiB of HBM per device.

v0:
```python
import jax
import jax.numpy as jnp
from jax import lax
from jax.sharding import PartitionSpec as P

BLOCK = 128


def swiglu_back(gate_sum, up_sum, hidden_grad):
    sigmoid = jax.nn.sigmoid(gate_sum)
    active = gate_sum * sigmoid
    hidden = active * up_sum
    silu_slope = sigmoid * (1.0 + gate_sum * (1.0 - sigmoid))
    gate_grad = hidden_grad * up_sum * silu_slope
    up_grad = hidden_grad * active
    return (gate_grad, up_grad, hidden)


def listed_tiles(left_rows, right_rows, block_ids, block_edge):
    row_count = left_rows.shape[0]
    per_row = right_rows.shape[1] // block_edge
    left_tiles = jnp.take(
        left_rows.reshape(row_count, -1, block_edge), block_ids // per_row, axis=1
    )
    right_tiles = jnp.take(
        right_rows.reshape(row_count, -1, block_edge), block_ids % per_row, axis=1
    )
    return jnp.einsum(
        "tsa,tsb->sab",
        left_tiles.astype(jnp.float32),
        right_tiles.astype(jnp.float32),
        precision=lax.Precision.HIGHEST,
    )


def finish(tiles, live_count, tile_scale):
    live_slots = jnp.arange(tiles.shape[0], dtype=jnp.int32) < live_count
    return jnp.where(live_slots[:, None, None], tiles * tile_scale, jnp.zeros_like(tiles))[
        None, None
    ]


def body(
    tokens,
    grad_out,
    gate_weight,
    up_weight,
    down_weight,
    gate_blocks,
    up_blocks,
    down_blocks,
    block_counts,
):
    contract = (((1,), (1,)), ((), ()))
    tokens_all, grads_all = (
        lax.all_gather(tokens, "row", axis=0, tiled=True),
        lax.all_gather(grad_out, "row", axis=0, tiled=True),
    )
    gate_part = jnp.dot(tokens_all, gate_weight, preferred_element_type=jnp.float32)
    up_part = jnp.dot(tokens_all, up_weight, preferred_element_type=jnp.float32)
    hidden_part = lax.dot_general(
        grads_all, down_weight, contract, preferred_element_type=jnp.float32
    )
    gate_sum, up_sum, hidden_grad = lax.psum((gate_part, up_part, hidden_part), "col")
    gate_grad, up_grad, hidden = swiglu_back(gate_sum, up_sum, hidden_grad)
    gate_low = gate_grad.astype(jnp.bfloat16)
    up_low = up_grad.astype(jnp.bfloat16)
    grad_in = lax.psum_scatter(
        lax.dot_general(gate_low, gate_weight, contract, preferred_element_type=jnp.float32)
        + lax.dot_general(up_low, up_weight, contract, preferred_element_type=jnp.float32),
        "row",
        scatter_dimension=0,
        tiled=True,
    )
    tile_scale = tokens_all.shape[0] ** (-0.5)
    counts = block_counts[0, 0]
    gate_tiles = listed_tiles(tokens_all, gate_grad, gate_blocks[0, 0], BLOCK)
    up_tiles = listed_tiles(tokens_all, up_grad, up_blocks[0, 0], BLOCK)
    down_tiles = listed_tiles(hidden, grads_all, down_blocks[0, 0], BLOCK)
    return (
        grad_in,
        finish(gate_tiles, counts[0], tile_scale),
        finish(up_tiles, counts[1], tile_scale),
        finish(down_tiles, counts[2], tile_scale),
    )


def solution(mesh):
    in_specs = (
        P("row", "col"),
        P("row", "col"),
        P("col", "row"),
        P("col", "row"),
        P("row", "col"),
        P("row", "col", None),
        P("row", "col", None),
        P("row", "col", None),
        P("row", "col", None),
    )
    out_specs = (
        P("row", "col"),
        P("row", "col", None, None, None),
        P("row", "col", None, None, None),
        P("row", "col", None, None, None),
    )
    return jax.shard_map(body, mesh=mesh, in_specs=in_specs, out_specs=out_specs, check_vma=False)
```

profile of v0, /device:TPU:16, one launch (start us, length us, event | category | flops | bytes accessed | tf_op | source)
XLA Modules:
  0.0 1006.6 jit_solution(5754072954942298145)
XLA Ops:
  7.2 0.0 copy-start
  7.2 0.0 copy-start.10
  7.2 0.0 all-gather.5.cloned.1.call-start
  7.2 0.7 all-gather.5.cloned.1.call-update
  7.9 0.0 all-gather.3.cloned.1.call-start
  8.0 0.7 all-gather.3.cloned.1.call-update
  8.7 0.0 copy-start.13
  8.7 0.0 all-reduce.3.cloned.1.call-start
  8.7 125.0 %all-gather.5.cloned.1.call-done = bf16[512,1024]{1,0:T(8,128)(2,1)} async-done(((bf16[8,1024]{1,0:T(8,128)(2,1)}), bf16[512,1024]{1,0:T(8,128)(2,1)}) %all-gather.5.cloned.1.call-update) | async-done | bytes 1048592 | tf_op jit(solution)/shard_map/all_gather | solution.py:56
  133.8 0.0 copy-done
  133.8 0.0 copy-start.1
  133.8 2.5 fusion.69
  136.3 0.0 copy-done.10
  136.3 0.0 copy-done.1
  136.3 1.2 fusion.68
  137.6 113.3 %all-gather.3.cloned.1.call-done = bf16[512,1024]{1,0:T(8,128)(2,1)} async-done(((bf16[8,1024]{1,0:T(8,128)(2,1)}), bf16[512,1024]{1,0:T(8,128)(2,1)}) %all-gather.3.cloned.1.call-update) | async-done | bytes 1048592 | tf_op jit(solution)/shard_map/all_gather | solution.py:57
  250.9 0.0 copy-done.13
  250.9 2.5 fusion.67
  253.4 0.0 all-reduce.3.cloned.1.call-update
  253.4 0.0 reduce-scatter.2.cloned.1.call-start
  253.5 302.8 %all-reduce.3.cloned.1.call-done = (f32[512,256]{1,0:T(8,128)}, f32[512,256]{1,0:T(8,128)}, f32[512,256]{1,0:T(8,128)}) async-done(((f32[512,256]{1,0:T(8,128)}, f32[512,256]{1,0:T(8,128)}, f32[512,256]{1,0:T(8,128)}), (f32[512,256]{1,0:T(8,128)}, f32[512,256]{1,0:T(8,128)}, f32[512,256]{1,0:T(8,128)})) %all-reduce.3.cloned.1.call-update) | async-done | bytes 1572880 | tf_op jit(solution)/shard_map/psum | solution.py:64
  556.2 2.6 multiply_bitcast_fusion
  558.8 0.0 copy-start.11
  558.8 0.0 copy-start.12
  558.8 0.5 fusion.56
  559.3 0.6 copy-done.11
  559.9 0.2 copy-done.12
  560.0 1.8 convolution_add_fusion
  561.9 0.0 copy-start.14
  561.9 0.0 reduce-scatter.2.cloned.1.call-update
  561.9 0.6 copy-done.14
  562.5 0.7 fusion.66
  563.2 0.6 iota_compare_fusion.2
  563.8 0.7 iota_compare_fusion.1
  564.5 0.7 iota_compare_fusion
  565.2 0.0 copy-done.15
  565.2 0.0 copy-done.16
  565.3 0.0 copy-done.17
  565.3 0.5 copy.30
  565.9 0.7 copy.31
  566.5 0.0 copy-start.7
  566.6 1.7 gather_fusion
  568.2 1.7 gather_fusion.2
  569.9 0.0 copy-done.7
  569.9 1.3 copy.38
  571.3 1.6 copy.39
  572.9 1.6 gather_fusion.5
  574.6 0.0 copy-start.8
  574.6 0.0 copy-start.9
  574.6 2.1 gather_fusion.1
  576.7 0.0 copy-done.8
  576.7 0.0 copy-done.9
  576.7 0.1 copy_bitcast_fusion
  576.7 2.1 gather_fusion.3
  578.8 2.0 gather_fusion.4
  580.8 0.0 copy-done.2
  580.8 3.8 fusion.33
  584.6 0.0 copy-done.4
  584.6 0.0 copy-done.5
  584.6 2.5 fusion.27
  587.1 0.0 copy-done.3
  587.1 0.0 copy-done.6
  587.1 2.7 fusion.21
  589.8 410.3 %reduce-scatter.2.cloned.1.call-done = f32[8,1024]{1,0:T(8,128)} async-done(((f32[512,1024]{1,0:T(8,128)}), f32[8,1024]{1,0:T(8,128)}) %reduce-scatter.2.cloned.1.call-update) | async-done | bytes 32784 | tf_op jit(solution)/shard_map/reduce_scatter | solution.py:68
  (15 shorter events, 0.1 us)
Async XLA Ops:
  7.2 126.6 %copy-start = (bf16[1024,256]{1,0:T(8,128)(2,1)S(1)}, bf16[1024,256]{1,0:T(8,128)(2,1)}, u32[]{:S(2)}) copy-start(bf16[1024,256]{1,0:T(8,128)(2,1)} %param.15) | copy-start | bytes 1572868
  7.2 129.1 %copy-start.10 = (bf16[1024,256]{1,0:T(8,128)(2,1)S(1)}, bf16[1024,256]{1,0:T(8,128)(2,1)}, u32[]{:S(2)}) copy-start(bf16[1024,256]{1,0:T(8,128)(2,1)} %param.16) | copy-start | bytes 1572868
  7.2 126.6 %all-gather.5.cloned.1.call-start = ((), (), s32[]{:S(2)}) async-start(), calls=%async_computation.2 | async-start | bytes 1064960 | tf_op jit(solution)/shard_map/all_gather | solution.py:56
  7.9 243.0 %all-gather.3.cloned.1.call-start = ((), (), s32[]{:S(2)}) async-start(), calls=%async_computation.1 | async-start | bytes 1064960 | tf_op jit(solution)/shard_map/all_gather | solution.py:57
  8.7 242.2 %copy-start.13 = (bf16[256,1024]{1,0:T(8,128)(2,1)S(1)}, bf16[256,1024]{1,0:T(8,128)(2,1)}, u32[]{:S(2)}) copy-start(bf16[256,1024]{1,0:T(8,128)(2,1)} %param.17) | copy-start | bytes 1572868
  8.7 547.6 %all-reduce.3.cloned.1.call-start = ((), (), s32[]{:S(2)}) async-start(), calls=%async_computation.4 | async-start | bytes 3145728 | tf_op jit(solution)/shard_map/psum | solution.py:64
  133.8 2.6 copy-start.1
  253.4 746.6 %reduce-scatter.2.cloned.1.call-start = ((), (), s32[]{:S(2)}) async-start(), calls=%async_computation.3 | async-start | bytes 2129920 | tf_op jit(solution)/shard_map/reduce_scatter | solution.py:68
  558.8 1.0 copy-start.11
  558.8 1.2 copy-start.12
  561.9 0.7 copy-start.14
  561.9 3.3 copy-start.15
  561.9 3.4 copy-start.16
  561.9 3.4 copy-start.17
  566.5 3.4 copy-start.7
  574.6 2.1 copy-start.8
  574.6 2.1 copy-start.9
  578.8 2.0 copy-start.2
  580.8 3.8 copy-start.4
  580.8 3.8 copy-start.5
  584.6 2.5 copy-start.3
  584.6 2.5 copy-start.6
Sparse Core Ops, SparseCore 0:
  10.2 123.5 all-gather.4
  135.9 114.9 all-gather.2
  254.7 301.5 all-reduce.2
  562.0 437.9 reduce-scatter.1
where the time goes:
time: 1010 us
  waiting for transfers between devices  953 us (94%)
  matrix products  17.6 us (2%)
  local copies, waits for them, and re-layouts  17.5 us (2%)
  between operations  14 us (1%)
    reduce_scatter x1, waiting for transfers between devices, body(): lax.psum_scatter(lax.dot_general(gate_low, gate_weight, contract, preferr...  410 us
    psum x1, waiting for transfers between devices, body(): lax.psum((gate_part, up_part, hidden_part), 'col')  303 us
    all_gather x1, waiting for transfers between devices, body(): lax.all_gather(tokens, 'row', axis=0, tiled=True)  125 us
    all_gather x1, waiting for transfers between devices, body(): lax.all_gather(grad_out, 'row', axis=0, tiled=True)  113 us
  transfers between devices with their start and end apart: 4, of which 4 were waited for; matrix products, arithmetic and copies ran while one was open for 3% of the time, Pallas kernels for 0%

commit v1 on v0

v1 whole, which is shorter than its diff:
```python
import jax
import jax.numpy as jnp
from jax import lax
from jax.experimental import pallas as pl
from jax.experimental.pallas import tpu as pltpu
from jax.sharding import PartitionSpec as P

BLOCK = 128
NZ, NX, NC = 8, 4, 2
NY, NH = 4, 2
CODE_TOP = 32000.0
PER_OCTAVE = 128.0
CODE_ROWS = 8
NT = (((1,), (1,)), ((), ()))
TN = (((0,), (0,)), ((), ()))
BF16, F32, I16, I32 = jnp.bfloat16, jnp.float32, jnp.int16, jnp.int32

Z_GROUPS = [[z * NX * NC + w for z in range(NZ)] for w in range(NX * NC)]
X_GROUPS = [[(z * NX + x) * NC + c for x in range(NX)] for z in range(NZ) for c in range(NC)]
Y_GROUPS = [[y * NH + h for y in range(NY)] for h in range(NH)]
CORE_SWAP = [(r, r ^ 1) for r in range(NZ * NX * NC)]
H_SWAP = [(c, c ^ 1) for c in range(NY * NH)]


def encode(values):
    top = jnp.max(jnp.abs(values), axis=0, keepdims=True)
    level = jnp.ceil(jnp.log2(jnp.maximum(top, 1e-30)) * PER_OCTAVE) + 1.0
    codes = jnp.round(values * (jnp.exp2(level * (-1.0 / PER_OCTAVE)) * CODE_TOP))
    rows = jnp.concatenate([codes, jnp.broadcast_to(level, (CODE_ROWS, values.shape[1]))], axis=0)
    return rows.astype(I32).astype(I16)


def decode(coded):
    rows = coded.astype(I32).astype(F32)
    count = rows.shape[0] - CODE_ROWS
    level = rows[count : count + 1]
    return rows[:count] * (jnp.exp2(level * (1.0 / PER_OCTAVE)) * (1.0 / CODE_TOP))


def project_tokens(tokens, gate_own, gate_sib, up_own, up_sib, out):
    rows = tokens[...].reshape(-1, tokens.shape[-1])
    per = tokens.shape[1]
    for k, weight in enumerate((gate_own, gate_sib, up_own, up_sib)):
        width = weight.shape[1]
        sums = jnp.dot(rows, weight[...], preferred_element_type=F32)
        for j in range(NY):
            out[j, :, k * width : (k + 1) * width] = encode(sums[j * per : (j + 1) * per])


def project_grads(grads, down_own, down_sib, out):
    rows = grads[...].reshape(-1, grads.shape[-1])
    per = grads.shape[1]
    for k, weight in enumerate((down_own, down_sib)):
        width = weight.shape[0]
        sums = lax.dot_general(rows, weight[...], NT, preferred_element_type=F32)
        for j in range(NY):
            out[j, :, k * width : (k + 1) * width] = encode(sums[j * per : (j + 1) * per])


def add_parts(parts, total, coded):
    value = decode(parts[0])
    for j in range(1, NY):
        value = value + decode(parts[j])
    total[...] = value
    coded[...] = encode(value)


def swiglu_kernel(gu_sum, gu_coded, hg_sum, hg_coded, low, hidden_low):
    half = hg_sum.shape[1]
    gate_up = gu_sum[...] + decode(gu_coded[...])
    hidden_grad = hg_sum[...] + decode(hg_coded[...])
    gate, up = gate_up[:, :half], gate_up[:, half:]
    sigmoid = 1.0 / (1.0 + jnp.exp(-gate))
    active = gate * sigmoid
    slope = sigmoid * (1.0 + gate * (1.0 - sigmoid))
    gate_grad = (hidden_grad * up * slope).astype(BF16)
    up_grad = (hidden_grad * active).astype(BF16)
    hidden = (active * up).astype(BF16)
    for j in range(NY):
        low[j, :, :half] = gate_grad
        low[j, :, half:] = up_grad
        hidden_low[j] = hidden


def input_grad(low, gate_own, gate_sib, up_own, up_sib, out):
    rows = low[...].reshape(-1, low.shape[-1])
    width = gate_own.shape[1]
    total = None
    for k, weight in enumerate((gate_own, gate_sib, up_own, up_sib)):
        part = lax.dot_general(
            rows[:, k * width : (k + 1) * width], weight[...], NT, preferred_element_type=F32
        )
        total = part if total is None else total + part
    out[...] = total.astype(BF16).reshape(out.shape)


def add_rows(parts, out):
    value = parts[0].astype(F32)
    for j in range(1, parts.shape[0]):
        value = value + parts[j].astype(F32)
    out[...] = value.astype(out.dtype)


def delta_kernel(
    gate_ids, up_ids, down_ids, counts,
    tok_own, tok_sib, grd_own, grd_sib, low_own, low_sib, hid_own, hid_sib,
    gate_out, up_out, down_out,
):
    scale = (2 * tok_own.shape[0]) ** (-0.5)
    width = low_sib.shape[1] // 2

    def tile(ref, start):
        return ref[:, pl.ds(pl.multiple_of(start, BLOCK), BLOCK)]

    def pair(left_own, left_sib, left, right_own, right_sib, right, right_sib_at):
        first = lax.dot_general(tile(left_own, left), tile(right_own, right), TN, preferred_element_type=F32)
        second = lax.dot_general(tile(left_sib, left), tile(right_sib, right_sib_at), TN, preferred_element_type=F32)
        return (first + second) * scale

    for s in range(gate_out.shape[0]):
        live = s < counts[0]

        @pl.when(live)
        def _():
            b = gate_ids[s]
            left, right = (b // 2) * BLOCK, (b % 2) * BLOCK
            gate_out[s] = pair(tok_own, tok_sib, left, low_own, low_sib, right, right)

        @pl.when(jnp.logical_not(live))
        def _():
            gate_out[s] = jnp.zeros((BLOCK, BLOCK), F32)

    for s in range(up_out.shape[0]):
        live = s < counts[1]

        @pl.when(live)
        def _():
            b = up_ids[s]
            left, right = (b // 2) * BLOCK, (b % 2) * BLOCK
            up_out[s] = pair(tok_own, tok_sib, left, low_own, low_sib, right + 2 * width, right + width)

        @pl.when(jnp.logical_not(live))
        def _():
            up_out[s] = jnp.zeros((BLOCK, BLOCK), F32)

    for s in range(down_out.shape[0]):
        live = s < counts[2]

        @pl.when(live)
        def _():
            b = down_ids[s]
            left, right = (b // 8) * BLOCK, (b % 8) * BLOCK
            down_out[s] = pair(hid_own, hid_sib, left, grd_own, grd_sib, right, right)

        @pl.when(jnp.logical_not(live))
        def _():
            down_out[s] = jnp.zeros((BLOCK, BLOCK), F32)


VMEM = pl.BlockSpec(memory_space=pltpu.VMEM)
SMEM = pl.BlockSpec(memory_space=pltpu.SMEM)


def call(kernel, outs, *args, specs=None):
    shapes = [jax.ShapeDtypeStruct(s, d) for s, d in outs]
    single = len(shapes) == 1
    return pl.pallas_call(
        kernel,
        out_shape=shapes[0] if single else shapes,
        in_specs=specs or [VMEM] * len(args),
        out_specs=VMEM if single else [VMEM] * len(shapes),
        compiler_params=pltpu.CompilerParams(vmem_limit_bytes=40 * 1024 * 1024),
    )(*args)


def spread(values, axis, groups):
    count = len(groups[0])
    return lax.all_to_all(
        jnp.broadcast_to(values[None], (count,) + values.shape), axis, 0, 0, axis_index_groups=groups
    )


def body(tokens, grad_out, gate_w, up_w, down_w, gate_blocks, up_blocks, down_blocks, block_counts):
    rows, width = tokens.shape
    hid = gate_w.shape[1]
    part = NZ * rows
    half = NX * part

    def gather(v):
        v = spread(v, "row", Z_GROUPS).reshape(part, width)
        return spread(v, "row", X_GROUPS)

    def swap(v):
        return lax.ppermute(v, "row", CORE_SWAP)

    tok, grd = gather(tokens), gather(grad_out)
    gate_s, up_s, down_s = swap(gate_w), swap(up_w), swap(down_w)

    coded = part + CODE_ROWS

    def col_sum(v):
        v = lax.all_to_all(v, "col", 0, 0, axis_index_groups=Y_GROUPS)
        total, code = call(add_parts, [((part, v.shape[2]), F32), (v.shape[1:], I16)], v)
        return total, lax.ppermute(code, "col", H_SWAP)

    gu = col_sum(call(project_tokens, [((NY, coded, 4 * hid), I16)], tok, gate_w, gate_s, up_w, up_s))
    hg = col_sum(call(project_grads, [((NY, coded, 2 * hid), I16)], grd, down_w, down_s))
    low, hidden = call(
        swiglu_kernel, [((NY, part, 4 * hid), BF16), ((NY, part, 2 * hid), BF16)], *gu, *hg
    )
    low = lax.all_to_all(low, "col", 0, 0, axis_index_groups=Y_GROUPS)
    hidden = lax.all_to_all(hidden, "col", 0, 0, axis_index_groups=Y_GROUPS)

    grad = call(input_grad, [((NX, part, width), BF16)], low, gate_w, gate_s, up_w, up_s)
    grad = lax.all_to_all(grad, "row", 0, 0, axis_index_groups=X_GROUPS)
    grad = call(add_rows, [((part, width), BF16)], grad).reshape(NZ, rows, width)
    grad = lax.all_to_all(grad, "row", 0, 0, axis_index_groups=Z_GROUPS)
    grad = call(add_rows, [((rows, width), F32)], grad)

    tok, grd = tok.reshape(half, width), grd.reshape(half, width)
    low, hidden = low.reshape(half, 4 * hid), hidden.reshape(half, 2 * hid)
    low_s = swap(jnp.concatenate([low[:, hid : 2 * hid], low[:, 3 * hid :]], axis=1))
    hidden_s = swap(hidden[:, hid:])
    tile = ((gate_blocks.shape[-1], BLOCK, BLOCK), F32)
    deltas = call(
        delta_kernel, [tile] * 3,
        gate_blocks[0, 0], up_blocks[0, 0], down_blocks[0, 0], block_counts[0, 0],
        tok, swap(tok), grd, swap(grd), low, low_s, hidden, hidden_s,
        specs=[SMEM] * 4 + [VMEM] * 8,
    )
    return (grad, *(d[None, None] for d in deltas))


def solution(mesh):
    two, three = P("row", "col"), P("row", "col", None)
    in_specs = (two, two, P("col", "row"), P("col", "row"), two, three, three, three, three)
    tiles = P("row", "col", None, None, None)
    return jax.shard_map(
        body, mesh=mesh, in_specs=in_specs, out_specs=(two, tiles, tiles, tiles), check_vma=False
    )
```

time: 1010 us -> 170 us (0.17)
  the two profiles are of different devices: /device:TPU:16 before, /device:TPU:1 now
where the time goes in v1:
time: 170 us; the launch traced here: 169 us
  starting transfers between devices  68.2 us (40%)
  blocking collectives  66.7 us (39%)
  waiting for transfers between devices  16.4 us (10%)
  Pallas kernels  13.7 us (8%)
  local copies, waits for them, and re-layouts  3.19 us (2%)
    all_to_all x2, blocking collectives, spread(): lax.all_to_all(jnp.broadcast_to(values[None], (count,) + values.shape), a...  38.9 us
    ppermute x7, starting transfers between devices, swap(): return lax.ppermute(v, 'row', CORE_SWAP)  26.5 us
    all_to_all x1, blocking collectives, body(): grad = lax.all_to_all(grad, 'row', 0, 0, axis_index_groups=X_GROUPS)  16.7 us
    ppermute x2, starting transfers between devices, col_sum(): return (total, lax.ppermute(code, 'col', H_SWAP))  14 us
    pallas_call x9, Pallas kernels, call(): pl.pallas_call(kernel, out_shape=shapes[0] if single else shapes, in_spec...  13.7 us
    all_to_all x1, blocking collectives, body(): low = lax.all_to_all(low, 'col', 0, 0, axis_index_groups=Y_GROUPS)  11.1 us
    ppermute x2, waiting for transfers between devices, col_sum(): return (total, lax.ppermute(code, 'col', H_SWAP))  9.64 us
    all_to_all x2, starting transfers between devices, spread(): lax.all_to_all(jnp.broadcast_to(values[None], (count,) + values.shape), a...  8.34 us
  transfers between devices with their start and end apart: 15, of which 5 were waited for; matrix products, arithmetic and copies ran while one was open for 1% of the time, Pallas kernels for 7%

profile of v1, /device:TPU:1, one launch (start us, length us, event | category | flops | bytes accessed | tf_op | source)
XLA Modules:
  0.0 169.0 jit_solution(5553261400543018009)
XLA Ops:
  0.6 0.7 broadcast_in_dim.35
  1.4 0.0 copy-start.11
  1.4 23.2 %all_to_all.50 = bf16[8,8,1024]{2,1,0:T(8,128)(2,1)S(1)} all-to-all(bf16[8,8,1024]{2,1,0:T(8,128)(2,1)S(1)} %broadcast_in_dim.35), channel_id=1, replica_groups={{0,8,16,24,32,40,48,56},{1,9,17,25,33,41,49,57},{2,10,18,26,34,42,50,58..., dimensions={0} | all-to-all | bytes 262144 | tf_op jit(solution)/shard_map/all_to_all | solution.py:178
  24.6 0.0 copy-done.11
  24.6 15.7 %all_to_all.51 = bf16[8,8,1024]{2,1,0:T(8,128)(2,1)S(1)} all-to-all(bf16[8,8,1024]{2,1,0:T(8,128)(2,1)S(1)} %broadcast_in_dim.38), channel_id=1, replica_groups={{0,8,16,24,32,40,48,56},{1,9,17,25,33,41,49,57},{2,10,18,26,34,42,50,58..., dimensions={0} | all-to-all | bytes 262144 | tf_op jit(solution)/shard_map/all_to_all | solution.py:178
  40.3 0.9 broadcast_in_dim.37
  41.2 0.0 copy-start
  41.2 0.0 copy-start.1
  41.2 4.1 %all-to-all-start.1 = ((bf16[4,64,1024]{2,1,0:T(8,128)(2,1)}), bf16[4,64,1024]{2,1,0:T(8,128)(2,1)S(1)}, u32[]{:S(2)}, u32[]{:S(2)}) async-start(bf16[4,64,1024]{2,1,0:T(8,128)(2,1)} %broadcast_in_dim.37), calls=%async_computation.1 | async-start | bytes 1048576 | tf_op jit(solution)/shard_map/all_to_all | solution.py:178
  45.3 0.0 copy-done
  45.3 4.6 %collective-permute-start = (bf16[1024,256]{1,0:T(8,128)(2,1)S(1)}, bf16[1024,256]{1,0:T(8,128)(2,1)S(1)}, u32[]{:S(2)}, u32[]{:S(2)}) collective-permute-start(bf16[1024,256]{1,0:T(8,128)(2,1)S(1)} %copy-done), channel_id=1, source_target_pairs={{0,1},{1,0},{2,3},{3,2},{4,5},{5,4},{6,7},{7,6},{8,9},{9,8},{10,11... | collective-permute-start | bytes 1572872 | tf_op jit(solution)/shard_map/ppermute | solution.py:194
  50.0 0.0 copy-done.1
  50.0 1.9 %collective-permute-start.1 = (bf16[1024,256]{1,0:T(8,128)(2,1)S(1)}, bf16[1024,256]{1,0:T(8,128)(2,1)S(1)}, u32[]{:S(2)}, u32[]{:S(2)}) collective-permute-start(bf16[1024,256]{1,0:T(8,128)(2,1)S(1)} %copy-done.1), channel_id=1, source_target_pairs={{0,1},{1,0},{2,3},{3,2},{4,5},{5,4},{6,7},{7,6},{8,9},{9,8},{10,11... | collective-permute-start | bytes 1572872 | tf_op jit(solution)/shard_map/ppermute | solution.py:194
  51.9 0.3 all-to-all-done.1.tokens
  52.2 0.9 broadcast_in_dim.40
  53.1 4.2 %all-to-all-start.4 = ((bf16[4,64,1024]{2,1,0:T(8,128)(2,1)}), bf16[4,64,1024]{2,1,0:T(8,128)(2,1)S(1)}, u32[]{:S(2)}, u32[]{:S(2)}) async-start(bf16[4,64,1024]{2,1,0:T(8,128)(2,1)} %broadcast_in_dim.40), calls=%async_computation.4 | async-start | bytes 1048576 | tf_op jit(solution)/shard_map/all_to_all | solution.py:178
  57.3 5.1 %collective-permute-start.3 = (bf16[256,1024]{1,0:T(8,128)(2,1)}, bf16[256,1024]{1,0:T(8,128)(2,1)}, u32[]{:S(2)}, u32[]{:S(2)}) collective-permute-start(bf16[256,1024]{1,0:T(8,128)(2,1)} %down_own.1), channel_id=1, source_target_pairs={{0,1},{1,0},{2,3},{3,2},{4,5},{5,4},{6,7},{7,6},{8,9},{9,8},{10,11... | collective-permute-start | bytes 1572872 | tf_op jit(solution)/shard_map/ppermute | solution.py:194
  62.4 0.0 collective-permute-done.gate_sib
  62.4 0.0 copy-start.2
  62.4 0.0 collective-permute-done.1.up_sib
  62.4 0.0 copy-start.4
  62.4 1.6 shard_map.120
  64.0 0.0 copy-done.2
  64.0 0.0 copy-done.4
  64.0 0.2 all-to-all-done.4.grads
  64.2 4.3 %all-to-all-start.2 = ((s16[4,72,1024]{2,1,0:T(8,128)(2,1)}), s16[4,72,1024]{2,1,0:T(8,128)(2,1)S(1)}, u32[]{:S(2)}, u32[]{:S(2)}) async-start(s16[4,72,1024]{2,1,0:T(8,128)(2,1)} %shard_map.120), calls=%async_computation.2 | async-start | bytes 1179648 | tf_op jit(solution)/shard_map/all_to_all | solution.py:202
  68.5 0.0 collective-permute-done.3.down_sib
  68.5 0.0 copy-done.6
  68.6 2.3 %shard_map.122 = s16[4,72,512]{2,1,0:T(8,128)(2,1)} custom-call(bf16[4,64,1024]{2,1,0:T(8,128)(2,1)S(1)} %all-to-all-done.4.grads, bf16[256,1024]{1,0:T(8,128)(2,1)S(1)} %copy-done.6, bf16[256,1024]{1,0:T(8,128)(2,1)} %collective-permute-done.3.down_sib), custom_call_target="tpu_custom_call" | custom-call | tf_op jit(solution)/shard_map/pallas_call | solution.py:167
  70.9 5.0 %all-to-all-done.2.parts = s16[4,72,1024]{2,1,0:T(8,128)(2,1)S(1)} async-done(((s16[4,72,1024]{2,1,0:T(8,128)(2,1)}), s16[4,72,1024]{2,1,0:T(8,128)(2,1)S(1)}, u32[]{:S(2)}, u32[]{:S(2)}) %all-to-all-start.2) | async-done | bytes 589856 | tf_op jit(solution)/shard_map/all_to_all | solution.py:202
  75.8 3.5 %all-to-all-start.5 = ((s16[4,72,512]{2,1,0:T(8,128)(2,1)}), s16[4,72,512]{2,1,0:T(8,128)(2,1)S(1)}, u32[]{:S(2)}, u32[]{:S(2)}) async-start(s16[4,72,512]{2,1,0:T(8,128)(2,1)} %shard_map.122), calls=%async_computation.5 | async-start | bytes 589824 | tf_op jit(solution)/shard_map/all_to_all | solution.py:202
  79.3 0.2 shard_map.121
  79.5 7.9 %collective-permute-start.2 = (s16[72,1024]{1,0:T(8,128)(2,1)S(1)}, s16[72,1024]{1,0:T(8,128)(2,1)S(1)}, u32[]{:S(2)}, u32[]{:S(2)}) collective-permute-start(s16[72,1024]{1,0:T(8,128)(2,1)S(1)} %get-tuple-element.14), channel_id=1, source_target_pairs={{0,64},{64,0},{128,192},{192,128},{256,320},{320,256},{384,448},{4... | collective-permute-start | bytes 442376 | tf_op jit(solution)/shard_map/ppermute | solution.py:204
  87.5 0.0 all-to-all-done.5.parts
  87.5 0.1 shard_map.123
  87.6 6.1 %collective-permute-start.4 = (s16[72,512]{1,0:T(8,128)(2,1)S(1)}, s16[72,512]{1,0:T(8,128)(2,1)S(1)}, u32[]{:S(2)}, u32[]{:S(2)}) collective-permute-start(s16[72,512]{1,0:T(8,128)(2,1)S(1)} %get-tuple-element.16), channel_id=1, source_target_pairs={{0,64},{64,0},{128,192},{192,128},{256,320},{320,256},{384,448},{4... | collective-permute-start | bytes 221192 | tf_op jit(solution)/shard_map/ppermute | solution.py:204
  93.7 9.6 %collective-permute-done.4.hg_coded = s16[72,512]{1,0:T(8,128)(2,1)S(1)} collective-permute-done((s16[72,512]{1,0:T(8,128)(2,1)S(1)}, s16[72,512]{1,0:T(8,128)(2,1)S(1)}, u32[]{:S(2)}, u32[]{:S(2)}) %collective-permute-start.4) | collective-permute-done | bytes 73760 | tf_op jit(solution)/shard_map/ppermute | solution.py:204
  103.3 0.0 collective-permute-done.2.gu_coded
  103.3 0.8 shard_map.124
  104.1 11.1 %all_to_all.52.low = bf16[4,64,1024]{2,1,0:T(8,128)(2,1)S(1)} all-to-all(bf16[4,64,1024]{2,1,0:T(8,128)(2,1)S(1)} %get-tuple-element.17), channel_id=1, replica_groups={{0,128,256,384},{64,192,320,448},{1,129,257,385},{65,193,321,449},{2,13..., dimensions={0} | all-to-all | bytes 1048576 | tf_op jit(solution)/shard_map/all_to_all | solution.py:211
  115.2 0.0 copy-done.3
  115.2 0.0 copy-done.5
  115.2 0.7 shard_map.125
  115.9 16.7 %all_to_all.53.parts = bf16[4,64,1024]{2,1,0:T(8,128)(2,1)S(1)} all-to-all(bf16[4,64,1024]{2,1,0:T(8,128)(2,1)S(1)} %shard_map.125), channel_id=1, replica_groups={{0,2,4,6},{1,3,5,7},{8,10,12,14},{9,11,13,15},{16,18,20,22},{17,19,21,2..., dimensions={0} | all-to-all | bytes 1048576 | tf_op jit(solution)/shard_map/all_to_all | solution.py:215
  132.6 3.4 %all-to-all-start.9 = ((bf16[4,64,512]{2,1,0:T(8,128)(2,1)}), bf16[4,64,512]{2,1,0:T(8,128)(2,1)S(1)}, u32[]{:S(2)}, u32[]{:S(2)}) async-start(bf16[4,64,512]{2,1,0:T(8,128)(2,1)} %get-tuple-element.18), calls=%async_computation.9 | async-start | bytes 524288 | tf_op jit(solution)/shard_map/all_to_all | solution.py:212
  136.0 6.7 %collective-permute-start.5 = (bf16[256,1024]{1,0:T(8,128)(2,1)S(1)}, bf16[256,1024]{1,0:T(8,128)(2,1)S(1)}, u32[]{:S(2)}, u32[]{:S(2)}) collective-permute-start(bf16[256,1024]{1,0:T(8,128)(2,1)S(1)} %bitcast.16), channel_id=1, source_target_pairs={{0,1},{1,0},{2,3},{3,2},{4,5},{5,4},{6,7},{7,6},{8,9},{9,8},{10,11... | collective-permute-start | bytes 1572872 | tf_op jit(solution)/shard_map/ppermute | solution.py:194
  142.7 1.9 %collective-permute-start.6 = (bf16[256,1024]{1,0:T(8,128)(2,1)S(1)}, bf16[256,1024]{1,0:T(8,128)(2,1)}, u32[]{:S(2)}, u32[]{:S(2)}) collective-permute-start(bf16[256,1024]{1,0:T(8,128)(2,1)S(1)} %bitcast.18), channel_id=1, source_target_pairs={{0,1},{1,0},{2,3},{3,2},{4,5},{5,4},{6,7},{7,6},{8,9},{9,8},{10,11... | collective-permute-start | bytes 1572872 | tf_op jit(solution)/shard_map/ppermute | solution.py:194
  144.7 0.7 shard_map.126
  145.4 0.0 all-to-all-done.9
  145.4 8.1 %all-to-all-start.8 = ((bf16[8,8,1024]{2,1,0:T(8,128)(2,1)}), bf16[8,8,1024]{2,1,0:T(8,128)(2,1)S(1)}, u32[]{:S(2)}, u32[]{:S(2)}) async-start(bf16[8,8,1024]{2,1,0:T(8,128)(2,1)} %bitcast.2), calls=%async_computation.8 | async-start | bytes 262144 | tf_op jit(solution)/shard_map/all_to_all | solution.py:217
  153.6 4.3 %collective-permute-start.7 = (bf16[256,512]{1,0:T(8,128)(2,1)S(1)}, bf16[256,512]{1,0:T(8,128)(2,1)S(1)}, u32[]{:S(2)}, u32[]{:S(2)}) collective-permute-start(bf16[256,512]{1,0:T(8,128)(2,1)S(1)} %pad_maximum_fusion), channel_id=1, source_target_pairs={{0,1},{1,0},{2,3},{3,2},{4,5},{5,4},{6,7},{7,6},{8,9},{9,8},{10,11... | collective-permute-start | bytes 786440 | tf_op jit(solution)/shard_map/ppermute | solution.py:194
  157.8 0.0 copy-start.10
  157.9 1.9 %collective-permute-start.8 = (bf16[256,256]{1,0:T(8,128)(2,1)S(1)}, bf16[256,256]{1,0:T(8,128)(2,1)S(1)}, u32[]{:S(2)}, u32[]{:S(2)}) collective-permute-start(bf16[256,256]{1,0:T(8,128)(2,1)S(1)} %slice.14), channel_id=1, source_target_pairs={{0,1},{1,0},{2,3},{3,2},{4,5},{5,4},{6,7},{7,6},{8,9},{9,8},{10,11... | collective-permute-start | bytes 393224 | tf_op jit(solution)/shard_map/ppermute | solution.py:194
  159.8 0.0 collective-permute-done.5.tok_sib
  159.8 0.0 collective-permute-done.6.grd_sib
  159.8 1.3 collective-permute-done.8.hid_sib
  161.1 0.0 collective-permute-done.7.low_sib
  161.1 0.0 copy-done.10
  161.1 0.6 copy-done.7
  161.8 0.0 copy-done.8
  161.8 0.0 copy-done.9
  161.8 6.6 %shard_map.128 = (f32[8,128,128]{2,1,0:T(8,128)}, f32[8,128,128]{2,1,0:T(8,128)}, f32[8,128,128]{2,1,0:T(8,128)}) custom-call(s32[8]{0:T(128)S(1)} %bitcast.22, s32[8]{0:T(128)S(1)} %bitcast.23, s32[8]{0:T(128)S(1)} %bitcast.24, s32[3]{0:T(128)S(1)} %bitcast.25, bf16[256,1024]{1,0:T(8,128)(2,1)S(1)} %bitcast.17, ...), custom_call_target="tpu_custom_call" | custom-call | tf_op jit(solution)/shard_map/pallas_call | solution.py:167
  168.4 0.0 all-to-all-done.8.parts
  168.4 0.6 shard_map.127
  (10 shorter events, 0.1 us)
Async XLA Ops:
  1.4 23.2 %copy-start.11 = (bf16[8,1024]{1,0:T(8,128)(2,1)S(1)}, bf16[8,1024]{1,0:T(8,128)(2,1)}, u32[]{:S(2)}) copy-start(bf16[8,1024]{1,0:T(8,128)(2,1)} %param.10) | copy-start | bytes 49156
  41.2 4.2 %copy-start = (bf16[1024,256]{1,0:T(8,128)(2,1)S(1)}, bf16[1024,256]{1,0:T(8,128)(2,1)}, u32[]{:S(2)}) copy-start(bf16[1024,256]{1,0:T(8,128)(2,1)} %gate_own.3) | copy-start | bytes 1572868
  41.2 8.8 %copy-start.1 = (bf16[1024,256]{1,0:T(8,128)(2,1)S(1)}, bf16[1024,256]{1,0:T(8,128)(2,1)}, u32[]{:S(2)}) copy-start(bf16[1024,256]{1,0:T(8,128)(2,1)} %up_own.3) | copy-start | bytes 1572868
  41.2 11.1 %all-to-all-start.1 = ((bf16[4,64,1024]{2,1,0:T(8,128)(2,1)}), bf16[4,64,1024]{2,1,0:T(8,128)(2,1)S(1)}, u32[]{:S(2)}, u32[]{:S(2)}) async-start(bf16[4,64,1024]{2,1,0:T(8,128)(2,1)} %broadcast_in_dim.37), calls=%async_computation.1 | async-start | bytes 1048576 | tf_op jit(solution)/shard_map/all_to_all | solution.py:178
  45.3 17.1 %collective-permute-start = (bf16[1024,256]{1,0:T(8,128)(2,1)S(1)}, bf16[1024,256]{1,0:T(8,128)(2,1)S(1)}, u32[]{:S(2)}, u32[]{:S(2)}) collective-permute-start(bf16[1024,256]{1,0:T(8,128)(2,1)S(1)} %copy-done), channel_id=1, source_target_pairs={{0,1},{1,0},{2,3},{3,2},{4,5},{5,4},{6,7},{7,6},{8,9},{9,8},{10,11... | collective-permute-start | bytes 1572872 | tf_op jit(solution)/shard_map/ppermute | solution.py:194
  50.0 12.4 %collective-permute-start.1 = (bf16[1024,256]{1,0:T(8,128)(2,1)S(1)}, bf16[1024,256]{1,0:T(8,128)(2,1)S(1)}, u32[]{:S(2)}, u32[]{:S(2)}) collective-permute-start(bf16[1024,256]{1,0:T(8,128)(2,1)S(1)} %copy-done.1), channel_id=1, source_target_pairs={{0,1},{1,0},{2,3},{3,2},{4,5},{5,4},{6,7},{7,6},{8,9},{9,8},{10,11... | collective-permute-start | bytes 1572872 | tf_op jit(solution)/shard_map/ppermute | solution.py:194
  53.1 11.1 %all-to-all-start.4 = ((bf16[4,64,1024]{2,1,0:T(8,128)(2,1)}), bf16[4,64,1024]{2,1,0:T(8,128)(2,1)S(1)}, u32[]{:S(2)}, u32[]{:S(2)}) async-start(bf16[4,64,1024]{2,1,0:T(8,128)(2,1)} %broadcast_in_dim.40), calls=%async_computation.4 | async-start | bytes 1048576 | tf_op jit(solution)/shard_map/all_to_all | solution.py:178
  57.3 11.3 %collective-permute-start.3 = (bf16[256,1024]{1,0:T(8,128)(2,1)}, bf16[256,1024]{1,0:T(8,128)(2,1)}, u32[]{:S(2)}, u32[]{:S(2)}) collective-permute-start(bf16[256,1024]{1,0:T(8,128)(2,1)} %down_own.1), channel_id=1, source_target_pairs={{0,1},{1,0},{2,3},{3,2},{4,5},{5,4},{6,7},{7,6},{8,9},{9,8},{10,11... | collective-permute-start | bytes 1572872 | tf_op jit(solution)/shard_map/ppermute | solution.py:194
  62.4 1.6 copy-start.2
  62.4 1.6 copy-start.4
  64.2 4.3 %copy-start.6 = (bf16[256,1024]{1,0:T(8,128)(2,1)S(1)}, bf16[256,1024]{1,0:T(8,128)(2,1)}, u32[]{:S(2)}) copy-start(bf16[256,1024]{1,0:T(8,128)(2,1)} %down_own.1) | copy-start | bytes 1572868
  64.2 11.6 %all-to-all-start.2 = ((s16[4,72,1024]{2,1,0:T(8,128)(2,1)}), s16[4,72,1024]{2,1,0:T(8,128)(2,1)S(1)}, u32[]{:S(2)}, u32[]{:S(2)}) async-start(s16[4,72,1024]{2,1,0:T(8,128)(2,1)} %shard_map.120), calls=%async_computation.2 | async-start | bytes 1179648 | tf_op jit(solution)/shard_map/all_to_all | solution.py:202
  75.8 11.6 %all-to-all-start.5 = ((s16[4,72,512]{2,1,0:T(8,128)(2,1)}), s16[4,72,512]{2,1,0:T(8,128)(2,1)S(1)}, u32[]{:S(2)}, u32[]{:S(2)}) async-start(s16[4,72,512]{2,1,0:T(8,128)(2,1)} %shard_map.122), calls=%async_computation.5 | async-start | bytes 589824 | tf_op jit(solution)/shard_map/all_to_all | solution.py:202
  79.5 23.8 %collective-permute-start.2 = (s16[72,1024]{1,0:T(8,128)(2,1)S(1)}, s16[72,1024]{1,0:T(8,128)(2,1)S(1)}, u32[]{:S(2)}, u32[]{:S(2)}) collective-permute-start(s16[72,1024]{1,0:T(8,128)(2,1)S(1)} %get-tuple-element.14), channel_id=1, source_target_pairs={{0,64},{64,0},{128,192},{192,128},{256,320},{320,256},{384,448},{4... | collective-permute-start | bytes 442376 | tf_op jit(solution)/shard_map/ppermute | solution.py:204
  87.6 15.7 %collective-permute-start.4 = (s16[72,512]{1,0:T(8,128)(2,1)S(1)}, s16[72,512]{1,0:T(8,128)(2,1)S(1)}, u32[]{:S(2)}, u32[]{:S(2)}) collective-permute-start(s16[72,512]{1,0:T(8,128)(2,1)S(1)} %get-tuple-element.16), channel_id=1, source_target_pairs={{0,64},{64,0},{128,192},{192,128},{256,320},{320,256},{384,448},{4... | collective-permute-start | bytes 221192 | tf_op jit(solution)/shard_map/ppermute | solution.py:204
  104.1 11.1 %copy-start.3 = (bf16[1024,256]{1,0:T(8,128)(2,1)S(1)}, bf16[1024,256]{1,0:T(8,128)(2,1)}, u32[]{:S(2)}) copy-start(bf16[1024,256]{1,0:T(8,128)(2,1)} %copy-done.2) | copy-start | bytes 1572868
  104.1 11.1 %copy-start.5 = (bf16[1024,256]{1,0:T(8,128)(2,1)S(1)}, bf16[1024,256]{1,0:T(8,128)(2,1)}, u32[]{:S(2)}) copy-start(bf16[1024,256]{1,0:T(8,128)(2,1)} %copy-done.4) | copy-start | bytes 1572868
  132.6 12.8 %all-to-all-start.9 = ((bf16[4,64,512]{2,1,0:T(8,128)(2,1)}), bf16[4,64,512]{2,1,0:T(8,128)(2,1)S(1)}, u32[]{:S(2)}, u32[]{:S(2)}) async-start(bf16[4,64,512]{2,1,0:T(8,128)(2,1)} %get-tuple-element.18), calls=%async_computation.9 | async-start | bytes 524288 | tf_op jit(solution)/shard_map/all_to_all | solution.py:212
  136.0 23.8 %collective-permute-start.5 = (bf16[256,1024]{1,0:T(8,128)(2,1)S(1)}, bf16[256,1024]{1,0:T(8,128)(2,1)S(1)}, u32[]{:S(2)}, u32[]{:S(2)}) collective-permute-start(bf16[256,1024]{1,0:T(8,128)(2,1)S(1)} %bitcast.16), channel_id=1, source_target_pairs={{0,1},{1,0},{2,3},{3,2},{4,5},{5,4},{6,7},{7,6},{8,9},{9,8},{10,11... | collective-permute-start | bytes 1572872 | tf_op jit(solution)/shard_map/ppermute | solution.py:194
  142.7 17.1 %collective-permute-start.6 = (bf16[256,1024]{1,0:T(8,128)(2,1)S(1)}, bf16[256,1024]{1,0:T(8,128)(2,1)}, u32[]{:S(2)}, u32[]{:S(2)}) collective-permute-start(bf16[256,1024]{1,0:T(8,128)(2,1)S(1)} %bitcast.18), channel_id=1, source_target_pairs={{0,1},{1,0},{2,3},{3,2},{4,5},{5,4},{6,7},{7,6},{8,9},{9,8},{10,11... | collective-permute-start | bytes 1572872 | tf_op jit(solution)/shard_map/ppermute | solution.py:194
  145.4 23.0 %all-to-all-start.8 = ((bf16[8,8,1024]{2,1,0:T(8,128)(2,1)}), bf16[8,8,1024]{2,1,0:T(8,128)(2,1)S(1)}, u32[]{:S(2)}, u32[]{:S(2)}) async-start(bf16[8,8,1024]{2,1,0:T(8,128)(2,1)} %bitcast.2), calls=%async_computation.8 | async-start | bytes 262144 | tf_op jit(solution)/shard_map/all_to_all | solution.py:217
  153.6 7.6 %collective-permute-start.7 = (bf16[256,512]{1,0:T(8,128)(2,1)S(1)}, bf16[256,512]{1,0:T(8,128)(2,1)S(1)}, u32[]{:S(2)}, u32[]{:S(2)}) collective-permute-start(bf16[256,512]{1,0:T(8,128)(2,1)S(1)} %pad_maximum_fusion), channel_id=1, source_target_pairs={{0,1},{1,0},{2,3},{3,2},{4,5},{5,4},{6,7},{7,6},{8,9},{9,8},{10,11... | collective-permute-start | bytes 786440 | tf_op jit(solution)/shard_map/ppermute | solution.py:194
  157.8 3.3 %copy-start.10 = (s32[1,1,3]{2,1,0:T(1,128)S(1)}, s32[1,1,3]{2,1,0:T(1,128)}, u32[]{:S(2)}) copy-start(s32[1,1,3]{2,1,0:T(1,128)} %param.17) | copy-start | bytes 40
  157.9 3.2 %collective-permute-start.8 = (bf16[256,256]{1,0:T(8,128)(2,1)S(1)}, bf16[256,256]{1,0:T(8,128)(2,1)S(1)}, u32[]{:S(2)}, u32[]{:S(2)}) collective-permute-start(bf16[256,256]{1,0:T(8,128)(2,1)S(1)} %slice.14), channel_id=1, source_target_pairs={{0,1},{1,0},{2,3},{3,2},{4,5},{5,4},{6,7},{7,6},{8,9},{9,8},{10,11... | collective-permute-start | bytes 393224 | tf_op jit(solution)/shard_map/ppermute | solution.py:194
  161.1 0.7 copy-start.7
  161.1 0.7 copy-start.8
  161.1 0.7 copy-start.9

commit v2 on v1

v2 whole, which is shorter than its diff:
```python
import jax
import jax.numpy as jnp
from jax import lax
from jax.experimental import pallas as pl
from jax.experimental.pallas import tpu as pltpu
from jax.sharding import PartitionSpec as P

BLOCK = 128
NZ, NX, NC = 8, 4, 2
NY, NH = 4, 2
CODE_TOP = 32000.0
PER_OCTAVE = 128.0
CODE_ROWS = 8
NT = (((1,), (1,)), ((), ()))
TN = (((0,), (0,)), ((), ()))
BF16, F32, I16, I32 = jnp.bfloat16, jnp.float32, jnp.int16, jnp.int32

Z_GROUPS = [[z * NX * NC + w for z in range(NZ)] for w in range(NX * NC)]
X_GROUPS = [[(z * NX + x) * NC + c for x in range(NX)] for z in range(NZ) for c in range(NC)]
Y_GROUPS = [[y * NH + h for y in range(NY)] for h in range(NH)]
CORE_SWAP = [(r, r ^ 1) for r in range(NZ * NX * NC)]
H_GROUPS = [[y * NH + h for h in range(NH)] for y in range(NY)]


def encode(values):
    top = jnp.max(jnp.abs(values), axis=0, keepdims=True)
    level = jnp.ceil(jnp.log2(jnp.maximum(top, 1e-30)) * PER_OCTAVE) + 1.0
    codes = jnp.round(values * (jnp.exp2(level * (-1.0 / PER_OCTAVE)) * CODE_TOP))
    rows = jnp.concatenate([codes, jnp.broadcast_to(level, (CODE_ROWS, values.shape[1]))], axis=0)
    return rows.astype(I32).astype(I16)


def decode(coded):
    rows = coded.astype(I32).astype(F32)
    count = rows.shape[0] - CODE_ROWS
    level = rows[count : count + 1]
    return rows[:count] * (jnp.exp2(level * (1.0 / PER_OCTAVE)) * (1.0 / CODE_TOP))


def project(acts, gate_own, gate_sib, up_own, up_sib, down_own, down_sib, out):
    per, width = acts.shape[1], acts.shape[2] // 2
    rows = acts[...].reshape(-1, 2 * width)
    tokens, grads = rows[:, :width], rows[:, width:]
    hid = gate_own.shape[1]

    def put(k, sums):
        for j in range(NY):
            out[j, :, k * hid : (k + 1) * hid] = encode(sums[j * per : (j + 1) * per])

    put(0, jnp.dot(tokens, gate_own[...], preferred_element_type=F32))
    put(1, jnp.dot(tokens, up_own[...], preferred_element_type=F32))
    put(2, lax.dot_general(grads, down_own[...], NT, preferred_element_type=F32))
    put(3, jnp.dot(tokens, gate_sib[...], preferred_element_type=F32))
    put(4, jnp.dot(tokens, up_sib[...], preferred_element_type=F32))
    put(5, lax.dot_general(grads, down_sib[...], NT, preferred_element_type=F32))


def add_parts(parts, coded):
    value = decode(parts[0])
    for j in range(1, NY):
        value = value + decode(parts[j])
    coded[...] = encode(value)


def swiglu_kernel(coded, low):
    values = decode(coded[0]) + decode(coded[1])
    hid = values.shape[1] // (3 * NC)
    for k in range(NC):
        at = 3 * k * hid
        gate, up, hidden_grad = (values[:, at + i * hid : at + (i + 1) * hid] for i in range(3))
        sigmoid = 1.0 / (1.0 + jnp.exp(-gate))
        active = gate * sigmoid
        slope = sigmoid * (1.0 + gate * (1.0 - sigmoid))
        results = (hidden_grad * up * slope, hidden_grad * active, active * up)
        for i, result in enumerate(results):
            low[:, at + i * hid : at + (i + 1) * hid] = result.astype(BF16)


def input_grad(low, gate_own, gate_sib, up_own, up_sib, out):
    rows = low[...].reshape(-1, low.shape[-1])
    hid = gate_own.shape[1]
    total = None
    for k, weight in ((0, gate_own), (1, up_own), (3, gate_sib), (4, up_sib)):
        part = lax.dot_general(
            rows[:, k * hid : (k + 1) * hid], weight[...], NT, preferred_element_type=F32
        )
        total = part if total is None else total + part
    out[...] = total.astype(BF16).reshape(out.shape)


def add_rows(parts, out):
    value = parts[0].astype(F32)
    for j in range(1, parts.shape[0]):
        value = value + parts[j].astype(F32)
    out[...] = value.astype(out.dtype)


def delta_kernel(
    gate_ids, up_ids, down_ids, counts, act_own, act_sib, low_own, low_sib, gate_out, up_out, down_out
):
    scale = (2 * act_own.shape[0]) ** (-0.5)
    width = act_own.shape[1] // 2
    hid = low_sib.shape[1] // 3

    def tile(ref, start):
        return ref[:, pl.ds(pl.multiple_of(start, BLOCK), BLOCK)]

    def pair(own, sib, left, right_own, right_sib, right):
        first = lax.dot_general(tile(own, left), tile(right_own, right), TN, preferred_element_type=F32)
        second = lax.dot_general(tile(sib, left), tile(right_sib, right), TN, preferred_element_type=F32)
        return (first + second) * scale

    def fill(out, count, compute):
        for s in range(out.shape[0]):
            live = s < count

            @pl.when(live)
            def _():
                out[s] = compute(s)

            @pl.when(jnp.logical_not(live))
            def _():
                out[s] = jnp.zeros((BLOCK, BLOCK), F32)

    def from_tokens(ids, base):
        def compute(s):
            b = ids[s]
            per = hid // BLOCK
            return pair(act_own, act_sib, (b // per) * BLOCK, low_own, low_sib, base + (b % per) * BLOCK)

        return compute

    def from_hidden(s):
        b = down_ids[s]
        per = width // BLOCK
        left, right = 2 * hid + (b // per) * BLOCK, width + (b % per) * BLOCK
        return pair(low_own, low_sib, left, act_own, act_sib, right)

    fill(gate_out, counts[0], from_tokens(gate_ids, 0))
    fill(up_out, counts[1], from_tokens(up_ids, hid))
    fill(down_out, counts[2], from_hidden)


VMEM = pl.BlockSpec(memory_space=pltpu.VMEM)
SMEM = pl.BlockSpec(memory_space=pltpu.SMEM)


def call(kernel, outs, *args, specs=None):
    shapes = [jax.ShapeDtypeStruct(s, d) for s, d in outs]
    single = len(shapes) == 1
    return pl.pallas_call(
        kernel,
        out_shape=shapes[0] if single else shapes,
        in_specs=specs or [VMEM] * len(args),
        out_specs=VMEM if single else [VMEM] * len(shapes),
        compiler_params=pltpu.CompilerParams(vmem_limit_bytes=16 * 1024 * 1024),
    )(*args)


def spread(values, axis, groups):
    count = len(groups[0])
    return lax.all_to_all(
        jnp.broadcast_to(values[None], (count,) + values.shape), axis, 0, 0, axis_index_groups=groups
    )


def body(tokens, grad_out, gate_w, up_w, down_w, gate_blocks, up_blocks, down_blocks, block_counts):
    rows, width = tokens.shape
    hid = gate_w.shape[1]
    part = NZ * rows
    half = NX * part
    cols = 3 * NC * hid

    def swap(v):
        return lax.ppermute(v, "row", CORE_SWAP)

    acts = spread(jnp.concatenate([tokens, grad_out], axis=1), "row", Z_GROUPS).reshape(part, 2 * width)
    acts, gate_s, up_s, down_s = lax.optimization_barrier((acts, swap(gate_w), swap(up_w), swap(down_w)))
    acts = spread(acts, "row", X_GROUPS)

    coded = part + CODE_ROWS
    sums = call(project, [((NY, coded, cols), I16)], acts, gate_w, gate_s, up_w, up_s, down_w, down_s)
    sums = lax.all_to_all(sums, "col", 0, 0, axis_index_groups=Y_GROUPS)
    acts = acts.reshape(half, 2 * width)
    code = call(add_parts, [((coded, cols), I16)], sums)
    code = lax.all_gather(code, "col", axis=0, axis_index_groups=H_GROUPS)
    low = call(swiglu_kernel, [((part, cols), BF16)], code)
    low = lax.all_gather(low, "col", axis=0, axis_index_groups=Y_GROUPS)

    grad = call(input_grad, [((NX, part, width), BF16)], low, gate_w, gate_s, up_w, up_s)
    grad = lax.all_to_all(grad, "row", 0, 0, axis_index_groups=X_GROUPS)
    low = low.reshape(half, cols)
    grad, low_s, acts_s = lax.optimization_barrier((grad, swap(low[:, cols // NC :]), swap(acts)))
    grad = call(add_rows, [((part, width), BF16)], grad).reshape(NZ, rows, width)
    grad = lax.all_to_all(grad, "row", 0, 0, axis_index_groups=Z_GROUPS)
    grad = call(add_rows, [((rows, width), F32)], grad)

    tile = ((gate_blocks.shape[-1], BLOCK, BLOCK), F32)
    deltas = call(
        delta_kernel, [tile] * 3,
        gate_blocks[0, 0], up_blocks[0, 0], down_blocks[0, 0], block_counts[0, 0],
        acts, acts_s, low, low_s,
        specs=[SMEM] * 4 + [VMEM] * 4,
    )
    return (grad, *(d[None, None] for d in deltas))


def solution(mesh):
    two, three = P("row", "col"), P("row", "col", None)
    in_specs = (two, two, P("col", "row"), P("col", "row"), two, three, three, three, three)
    tiles = P("row", "col", None, None, None)
    return jax.shard_map(
        body, mesh=mesh, in_specs=in_specs, out_specs=(two, tiles, tiles, tiles), check_vma=False
    )
```

time: 170 us -> 139 us (0.82)
  the two profiles are of different devices: /device:TPU:1 before, /device:TPU:2 now
where the time goes in v2:
time: 139 us; the launch traced here: 138 us
  blocking collectives  56.7 us (41%)
  starting transfers between devices  37.5 us (27%)
  waiting for transfers between devices  28.8 us (21%)
  Pallas kernels  10.5 us (8%)
  local copies, waits for them, and re-layouts  2.71 us (2%)
    all_gather x1, blocking collectives, body(): code = lax.all_gather(code, 'col', axis=0, axis_index_groups=H_GROUPS)  29.1 us
    all_to_all x1, blocking collectives, spread(): lax.all_to_all(jnp.broadcast_to(values[None], (count,) + values.shape), a...  14.2 us
    all_gather x1, blocking collectives, body(): low = lax.all_gather(low, 'col', axis=0, axis_index_groups=Y_GROUPS)  13.4 us
    all_to_all x1, starting transfers between devices, spread(): lax.all_to_all(jnp.broadcast_to(values[None], (count,) + values.shape), a...  12.5 us
    pallas_call x7, Pallas kernels, call(): pl.pallas_call(kernel, out_shape=shapes[0] if single else shapes, in_spec...  10.5 us
    ppermute x5, starting transfers between devices, swap(): return lax.ppermute(v, 'row', CORE_SWAP)  10.1 us
    all_to_all x1, waiting for transfers between devices, spread(): lax.all_to_all(jnp.broadcast_to(values[None], (count,) + values.shape), a...  8.31 us
    all_to_all x1, waiting for transfers between devices, body(): sums = lax.all_to_all(sums, 'col', 0, 0, axis_index_groups=Y_GROUPS)  8.1 us
  transfers between devices with their start and end apart: 9, of which 5 were waited for; matrix products, arithmetic and copies ran while one was open for 1% of the time, Pallas kernels for 5%

profile of v2, /device:TPU:2, one launch (start us, length us, event | category | flops | bytes accessed | tf_op | source)
XLA Modules:
  0.0 137.9 jit_solution(7417162686759975697)
XLA Ops:
  0.6 0.0 copy-start
  0.6 0.8 pad_maximum_fusion
  1.4 0.7 broadcast_in_dim.10
  2.2 12.5 %all-to-all-start = ((bf16[8,8,2048]{2,1,0:T(8,128)(2,1)}), bf16[8,8,2048]{2,1,0:T(8,128)(2,1)S(1)}, u32[]{:S(2)}, u32[]{:S(2)}) async-start(bf16[8,8,2048]{2,1,0:T(8,128)(2,1)} %broadcast_in_dim.10), calls=%async_computation | async-start | bytes 524288 | tf_op jit(solution)/shard_map/all_to_all | solution.py:162
  14.7 0.0 copy-done
  14.7 1.9 %collective-permute-start = (bf16[1024,256]{1,0:T(8,128)(2,1)S(1)}, bf16[1024,256]{1,0:T(8,128)(2,1)S(1)}, u32[]{:S(2)}, u32[]{:S(2)}) collective-permute-start(bf16[1024,256]{1,0:T(8,128)(2,1)S(1)} %copy-done), channel_id=1, source_target_pairs={{0,1},{1,0},{2,3},{3,2},{4,5},{5,4},{6,7},{7,6},{8,9},{9,8},{10,11... | collective-permute-start | bytes 1572872 | tf_op jit(solution)/shard_map/ppermute | solution.py:175
  16.6 2.4 %collective-permute-start.1 = (bf16[1024,256]{1,0:T(8,128)(2,1)}, bf16[1024,256]{1,0:T(8,128)(2,1)S(1)}, u32[]{:S(2)}, u32[]{:S(2)}) collective-permute-start(bf16[1024,256]{1,0:T(8,128)(2,1)} %up_own.3), channel_id=1, source_target_pairs={{0,1},{1,0},{2,3},{3,2},{4,5},{5,4},{6,7},{7,6},{8,9},{9,8},{10,11... | collective-permute-start | bytes 1572872 | tf_op jit(solution)/shard_map/ppermute | solution.py:175
  19.0 1.9 %collective-permute-start.2 = (bf16[256,1024]{1,0:T(8,128)(2,1)}, bf16[256,1024]{1,0:T(8,128)(2,1)S(1)}, u32[]{:S(2)}, u32[]{:S(2)}) collective-permute-start(bf16[256,1024]{1,0:T(8,128)(2,1)} %down_own.1), channel_id=1, source_target_pairs={{0,1},{1,0},{2,3},{3,2},{4,5},{5,4},{6,7},{7,6},{8,9},{9,8},{10,11... | collective-permute-start | bytes 1572872 | tf_op jit(solution)/shard_map/ppermute | solution.py:175
  21.0 0.0 collective-permute-done.gate_sib
  21.0 0.0 copy-start.3
  21.0 0.0 collective-permute-done.1.up_sib
  21.0 0.0 copy-start.5
  21.0 2.0 %collective-permute-done.2.down_sib = bf16[256,1024]{1,0:T(8,128)(2,1)S(1)} collective-permute-done((bf16[256,1024]{1,0:T(8,128)(2,1)}, bf16[256,1024]{1,0:T(8,128)(2,1)S(1)}, u32[]{:S(2)}, u32[]{:S(2)}) %collective-permute-start.2) | collective-permute-done | bytes 524320 | tf_op jit(solution)/shard_map/ppermute | solution.py:175
  23.1 8.3 %all-to-all-done = bf16[8,8,2048]{2,1,0:T(8,128)(2,1)S(1)} async-done(((bf16[8,8,2048]{2,1,0:T(8,128)(2,1)}), bf16[8,8,2048]{2,1,0:T(8,128)(2,1)S(1)}, u32[]{:S(2)}, u32[]{:S(2)}) %all-to-all-start) | async-done | bytes 262176 | tf_op jit(solution)/shard_map/all_to_all | solution.py:162
  31.4 0.1 broadcast_in_dim.22
  31.5 0.0 copy-start.1
  31.5 0.0 copy-start.7
  31.5 14.2 %all_to_all.25.acts = bf16[4,64,2048]{2,1,0:T(8,128)(2,1)S(1)} all-to-all(bf16[4,64,2048]{2,1,0:T(8,128)(2,1)S(1)} %broadcast_in_dim.22), channel_id=1, replica_groups={{0,2,4,6},{1,3,5,7},{8,10,12,14},{9,11,13,15},{16,18,20,22},{17,19,21,2..., dimensions={0} | all-to-all | bytes 2097152 | tf_op jit(solution)/shard_map/all_to_all | solution.py:162
  45.7 0.0 copy-done.3
  45.7 0.0 copy-done.5
  45.7 0.0 copy-done.1
  45.7 0.0 copy-done.7
  45.7 2.0 %shard_map.120 = s16[4,72,1536]{2,1,0:T(8,128)(2,1)} custom-call(bf16[4,64,2048]{2,1,0:T(8,128)(2,1)S(1)} %all_to_all.25.acts, bf16[1024,256]{1,0:T(8,128)(2,1)S(1)} %copy-done, bf16[1024,256]{1,0:T(8,128)(2,1)S(1)} %collective-permute-done.gate_sib, bf16[1024,256]{1,0:T(8,128)(2,1)S(1)} %copy-done.1, bf16[1024,256]{1,0:T(8,128)(2,1)S(1)} %collective-permute-done.1.up_sib, ...), custom_call_target="tpu_custom_call" | custom-call | tf_op jit(solution)/shard_map/pallas_call | solution.py:151
  47.7 4.5 %all-to-all-start.2 = ((s16[4,72,1536]{2,1,0:T(8,128)(2,1)}), s16[4,72,1536]{2,1,0:T(8,128)(2,1)S(1)}, u32[]{:S(2)}, u32[]{:S(2)}) async-start(s16[4,72,1536]{2,1,0:T(8,128)(2,1)} %shard_map.120), calls=%async_computation.2 | async-start | bytes 1769472 | tf_op jit(solution)/shard_map/all_to_all | solution.py:183
  52.2 1.9 %collective-permute-start.4 = (bf16[256,2048]{1,0:T(8,128)(2,1)S(1)}, bf16[256,2048]{1,0:T(8,128)(2,1)S(1)}, u32[]{:S(2)}, u32[]{:S(2)}) collective-permute-start(bf16[256,2048]{1,0:T(8,128)(2,1)S(1)} %bitcast.13), channel_id=1, source_target_pairs={{0,1},{1,0},{2,3},{3,2},{4,5},{5,4},{6,7},{7,6},{8,9},{9,8},{10,11... | collective-permute-start | bytes 3145736 | tf_op jit(solution)/shard_map/ppermute | solution.py:175
  54.1 8.1 %all-to-all-done.2.parts = s16[4,72,1536]{2,1,0:T(8,128)(2,1)S(1)} async-done(((s16[4,72,1536]{2,1,0:T(8,128)(2,1)}), s16[4,72,1536]{2,1,0:T(8,128)(2,1)S(1)}, u32[]{:S(2)}, u32[]{:S(2)}) %all-to-all-start.2) | async-done | bytes 884768 | tf_op jit(solution)/shard_map/all_to_all | solution.py:183
  62.2 0.3 shard_map.121
  62.5 29.1 %all-gather = s16[144,1536]{1,0:T(8,128)(2,1)S(1)} all-gather(s16[72,1536]{1,0:T(8,128)(2,1)S(1)} %shard_map.121), channel_id=2, replica_groups={{0,64},{128,192},{256,320},{384,448},{1,65},{129,193},{257,321},{385,44..., dimensions={0}, use_global_device_ids=true | all-gather | bytes 663552 | tf_op jit(solution)/shard_map/all_gather | solution.py:186
  91.6 0.2 shard_map.122
  91.8 0.0 copy-start.4
  91.8 0.0 copy-start.6
  91.8 13.4 %all-gather.1.low_own = bf16[256,1536]{1,0:T(8,128)(2,1)S(1)} all-gather(bf16[64,1536]{1,0:T(8,128)(2,1)S(1)} %shard_map.122), channel_id=3, replica_groups={{0,128,256,384},{64,192,320,448},{1,129,257,385},{65,193,321,449},{2,13..., dimensions={0}, use_global_device_ids=true | all-gather | bytes 983040 | tf_op jit(solution)/shard_map/all_gather | solution.py:188
  105.3 0.0 copy-start.2
  105.3 0.8 slice.4
  106.0 0.0 copy-done.4
  106.0 0.0 copy-done.6
  106.0 0.4 copy-done.2
  106.5 1.5 %shard_map.123 = bf16[4,64,1024]{2,1,0:T(8,128)(2,1)} custom-call(bf16[4,64,1536]{2,1,0:T(8,128)(2,1)S(1)} %bitcast.12, bf16[1024,256]{1,0:T(8,128)(2,1)S(1)} %copy-done, bf16[1024,256]{1,0:T(8,128)(2,1)S(1)} %copy-done.4, bf16[1024,256]{1,0:T(8,128)(2,1)S(1)} %copy-done.2, bf16[1024,256]{1,0:T(8,128)(2,1)S(1)} %copy-done.6), custom_call_target="tpu_custom_call" | custom-call | tf_op jit(solution)/shard_map/pallas_call | solution.py:151
  108.0 4.9 %all-to-all-start.3 = ((bf16[4,64,1024]{2,1,0:T(8,128)(2,1)}), bf16[4,64,1024]{2,1,0:T(8,128)(2,1)S(1)}, u32[]{:S(2)}, u32[]{:S(2)}) async-start(bf16[4,64,1024]{2,1,0:T(8,128)(2,1)} %shard_map.123), calls=%async_computation.3 | async-start | bytes 1048576 | tf_op jit(solution)/shard_map/all_to_all | solution.py:191
  112.9 1.9 %collective-permute-start.3 = (bf16[256,768]{1,0:T(8,128)(2,1)}, bf16[256,768]{1,0:T(8,128)(2,1)}, u32[]{:S(2)}, u32[]{:S(2)}) collective-permute-start(bf16[256,768]{1,0:T(8,128)(2,1)} %slice.4), channel_id=1, source_target_pairs={{0,1},{1,0},{2,3},{3,2},{4,5},{5,4},{6,7},{7,6},{8,9},{9,8},{10,11... | collective-permute-start | bytes 1179656 | tf_op jit(solution)/shard_map/ppermute | solution.py:175
  114.8 0.0 collective-permute-done.4.act_sib
  114.8 4.7 %all-to-all-done.3.parts = bf16[4,64,1024]{2,1,0:T(8,128)(2,1)S(1)} async-done(((bf16[4,64,1024]{2,1,0:T(8,128)(2,1)}), bf16[4,64,1024]{2,1,0:T(8,128)(2,1)S(1)}, u32[]{:S(2)}, u32[]{:S(2)}) %all-to-all-start.3) | async-done | bytes 524320 | tf_op jit(solution)/shard_map/all_to_all | solution.py:191
  119.5 0.0 collective-permute-done.3.low_sib
  119.5 0.7 shard_map.124
  120.2 0.0 copy-start.11
  120.2 5.6 %all-to-all-start.4 = ((bf16[8,8,1024]{2,1,0:T(8,128)(2,1)}), bf16[8,8,1024]{2,1,0:T(8,128)(2,1)S(1)}, u32[]{:S(2)}, u32[]{:S(2)}) async-start(bf16[8,8,1024]{2,1,0:T(8,128)(2,1)} %bitcast.4), calls=%async_computation.4 | async-start | bytes 262144 | tf_op jit(solution)/shard_map/all_to_all | solution.py:195
  125.8 0.0 copy-start.8
  125.8 0.0 copy-start.9
  125.8 0.0 copy-start.10
  125.8 0.0 copy-done.11
  125.8 0.6 copy-done.8
  126.5 0.0 copy-done.9
  126.5 0.0 copy-done.10
  126.5 5.1 %shard_map.126 = (f32[8,128,128]{2,1,0:T(8,128)}, f32[8,128,128]{2,1,0:T(8,128)}, f32[8,128,128]{2,1,0:T(8,128)}) custom-call(s32[8]{0:T(128)S(1)} %bitcast.16, s32[8]{0:T(128)S(1)} %bitcast.17, s32[8]{0:T(128)S(1)} %bitcast.18, s32[3]{0:T(128)S(1)} %bitcast.19, bf16[256,2048]{1,0:T(8,128)(2,1)S(1)} %bitcast.14, ...), custom_call_target="tpu_custom_call" | custom-call | tf_op jit(solution)/shard_map/pallas_call | solution.py:151
  131.6 5.6 %all-to-all-done.4.parts = bf16[8,8,1024]{2,1,0:T(8,128)(2,1)S(1)} async-done(((bf16[8,8,1024]{2,1,0:T(8,128)(2,1)}), bf16[8,8,1024]{2,1,0:T(8,128)(2,1)S(1)}, u32[]{:S(2)}, u32[]{:S(2)}) %all-to-all-start.4) | async-done | bytes 131104 | tf_op jit(solution)/shard_map/all_to_all | solution.py:195
  137.2 0.6 shard_map.125
Async XLA Ops:
  0.6 14.1 %copy-start = (bf16[1024,256]{1,0:T(8,128)(2,1)S(1)}, bf16[1024,256]{1,0:T(8,128)(2,1)}, u32[]{:S(2)}) copy-start(bf16[1024,256]{1,0:T(8,128)(2,1)} %gate_own.3) | copy-start | bytes 1572868
  2.2 29.2 %all-to-all-start = ((bf16[8,8,2048]{2,1,0:T(8,128)(2,1)}), bf16[8,8,2048]{2,1,0:T(8,128)(2,1)S(1)}, u32[]{:S(2)}, u32[]{:S(2)}) async-start(bf16[8,8,2048]{2,1,0:T(8,128)(2,1)} %broadcast_in_dim.10), calls=%async_computation | async-start | bytes 524288 | tf_op jit(solution)/shard_map/all_to_all | solution.py:162
  14.7 6.3 %collective-permute-start = (bf16[1024,256]{1,0:T(8,128)(2,1)S(1)}, bf16[1024,256]{1,0:T(8,128)(2,1)S(1)}, u32[]{:S(2)}, u32[]{:S(2)}) collective-permute-start(bf16[1024,256]{1,0:T(8,128)(2,1)S(1)} %copy-done), channel_id=1, source_target_pairs={{0,1},{1,0},{2,3},{3,2},{4,5},{5,4},{6,7},{7,6},{8,9},{9,8},{10,11... | collective-permute-start | bytes 1572872 | tf_op jit(solution)/shard_map/ppermute | solution.py:175
  16.6 4.4 %collective-permute-start.1 = (bf16[1024,256]{1,0:T(8,128)(2,1)}, bf16[1024,256]{1,0:T(8,128)(2,1)S(1)}, u32[]{:S(2)}, u32[]{:S(2)}) collective-permute-start(bf16[1024,256]{1,0:T(8,128)(2,1)} %up_own.3), channel_id=1, source_target_pairs={{0,1},{1,0},{2,3},{3,2},{4,5},{5,4},{6,7},{7,6},{8,9},{9,8},{10,11... | collective-permute-start | bytes 1572872 | tf_op jit(solution)/shard_map/ppermute | solution.py:175
  19.0 4.0 %collective-permute-start.2 = (bf16[256,1024]{1,0:T(8,128)(2,1)}, bf16[256,1024]{1,0:T(8,128)(2,1)S(1)}, u32[]{:S(2)}, u32[]{:S(2)}) collective-permute-start(bf16[256,1024]{1,0:T(8,128)(2,1)} %down_own.1), channel_id=1, source_target_pairs={{0,1},{1,0},{2,3},{3,2},{4,5},{5,4},{6,7},{7,6},{8,9},{9,8},{10,11... | collective-permute-start | bytes 1572872 | tf_op jit(solution)/shard_map/ppermute | solution.py:175
  21.0 24.7 %copy-start.3 = (bf16[1024,256]{1,0:T(8,128)(2,1)}, bf16[1024,256]{1,0:T(8,128)(2,1)S(1)}, u32[]{:S(2)}) copy-start(bf16[1024,256]{1,0:T(8,128)(2,1)S(1)} %collective-permute-done.gate_sib) | copy-start | bytes 1572868
  21.0 24.7 %copy-start.5 = (bf16[1024,256]{1,0:T(8,128)(2,1)}, bf16[1024,256]{1,0:T(8,128)(2,1)S(1)}, u32[]{:S(2)}) copy-start(bf16[1024,256]{1,0:T(8,128)(2,1)S(1)} %collective-permute-done.1.up_sib) | copy-start | bytes 1572868
  31.5 14.2 %copy-start.1 = (bf16[1024,256]{1,0:T(8,128)(2,1)S(1)}, bf16[1024,256]{1,0:T(8,128)(2,1)}, u32[]{:S(2)}) copy-start(bf16[1024,256]{1,0:T(8,128)(2,1)} %up_own.3) | copy-start | bytes 1572868
  31.5 14.2 %copy-start.7 = (bf16[256,1024]{1,0:T(8,128)(2,1)S(1)}, bf16[256,1024]{1,0:T(8,128)(2,1)}, u32[]{:S(2)}) copy-start(bf16[256,1024]{1,0:T(8,128)(2,1)} %down_own.1) | copy-start | bytes 1572868
  47.7 14.5 %all-to-all-start.2 = ((s16[4,72,1536]{2,1,0:T(8,128)(2,1)}), s16[4,72,1536]{2,1,0:T(8,128)(2,1)S(1)}, u32[]{:S(2)}, u32[]{:S(2)}) async-start(s16[4,72,1536]{2,1,0:T(8,128)(2,1)} %shard_map.120), calls=%async_computation.2 | async-start | bytes 1769472 | tf_op jit(solution)/shard_map/all_to_all | solution.py:183
  52.2 62.6 %collective-permute-start.4 = (bf16[256,2048]{1,0:T(8,128)(2,1)S(1)}, bf16[256,2048]{1,0:T(8,128)(2,1)S(1)}, u32[]{:S(2)}, u32[]{:S(2)}) collective-permute-start(bf16[256,2048]{1,0:T(8,128)(2,1)S(1)} %bitcast.13), channel_id=1, source_target_pairs={{0,1},{1,0},{2,3},{3,2},{4,5},{5,4},{6,7},{7,6},{8,9},{9,8},{10,11... | collective-permute-start | bytes 3145736 | tf_op jit(solution)/shard_map/ppermute | solution.py:175
  91.8 14.2 %copy-start.4 = (bf16[1024,256]{1,0:T(8,128)(2,1)S(1)}, bf16[1024,256]{1,0:T(8,128)(2,1)}, u32[]{:S(2)}) copy-start(bf16[1024,256]{1,0:T(8,128)(2,1)} %copy-done.3) | copy-start | bytes 1572868
  91.8 14.2 %copy-start.6 = (bf16[1024,256]{1,0:T(8,128)(2,1)S(1)}, bf16[1024,256]{1,0:T(8,128)(2,1)}, u32[]{:S(2)}) copy-start(bf16[1024,256]{1,0:T(8,128)(2,1)} %copy-done.5) | copy-start | bytes 1572868
  105.3 1.2 copy-start.2
  108.0 11.5 %all-to-all-start.3 = ((bf16[4,64,1024]{2,1,0:T(8,128)(2,1)}), bf16[4,64,1024]{2,1,0:T(8,128)(2,1)S(1)}, u32[]{:S(2)}, u32[]{:S(2)}) async-start(bf16[4,64,1024]{2,1,0:T(8,128)(2,1)} %shard_map.123), calls=%async_computation.3 | async-start | bytes 1048576 | tf_op jit(solution)/shard_map/all_to_all | solution.py:191
  112.9 6.6 %collective-permute-start.3 = (bf16[256,768]{1,0:T(8,128)(2,1)}, bf16[256,768]{1,0:T(8,128)(2,1)}, u32[]{:S(2)}, u32[]{:S(2)}) collective-permute-start(bf16[256,768]{1,0:T(8,128)(2,1)} %slice.4), channel_id=1, source_target_pairs={{0,1},{1,0},{2,3},{3,2},{4,5},{5,4},{6,7},{7,6},{8,9},{9,8},{10,11... | collective-permute-start | bytes 1179656 | tf_op jit(solution)/shard_map/ppermute | solution.py:175
  120.2 5.6 %copy-start.11 = (s32[1,1,3]{2,1,0:T(1,128)S(1)}, s32[1,1,3]{2,1,0:T(1,128)}, u32[]{:S(2)}) copy-start(s32[1,1,3]{2,1,0:T(1,128)} %param.17) | copy-start | bytes 40
  120.2 17.0 %all-to-all-start.4 = ((bf16[8,8,1024]{2,1,0:T(8,128)(2,1)}), bf16[8,8,1024]{2,1,0:T(8,128)(2,1)S(1)}, u32[]{:S(2)}, u32[]{:S(2)}) async-start(bf16[8,8,1024]{2,1,0:T(8,128)(2,1)} %bitcast.4), calls=%async_computation.4 | async-start | bytes 262144 | tf_op jit(solution)/shard_map/all_to_all | solution.py:195
  125.8 0.7 copy-start.8
  125.8 0.7 copy-start.9
  125.8 0.7 copy-start.10

commit v3 on v2

--- a/solution.py
+++ b/solution.py
@@ -10,7 +10,9 @@
 NY, NH = 4, 2
 CODE_TOP = 32000.0
 PER_OCTAVE = 128.0
-CODE_ROWS = 8
+LANES = 128
+BLOCKS = 12
+LEVEL_ROWS = 16
 NT = (((1,), (1,)), ((), ()))
 TN = (((0,), (0,)), ((), ()))
 BF16, F32, I16, I32 = jnp.bfloat16, jnp.float32, jnp.int16, jnp.int32
@@ -22,30 +24,47 @@
 H_GROUPS = [[y * NH + h for h in range(NH)] for y in range(NY)]
 
 
-def encode(values):
-    top = jnp.max(jnp.abs(values), axis=0, keepdims=True)
-    level = jnp.ceil(jnp.log2(jnp.maximum(top, 1e-30)) * PER_OCTAVE) + 1.0
-    codes = jnp.round(values * (jnp.exp2(level * (-1.0 / PER_OCTAVE)) * CODE_TOP))
-    rows = jnp.concatenate([codes, jnp.broadcast_to(level, (CODE_ROWS, values.shape[1]))], axis=0)
-    return rows.astype(I32).astype(I16)
+def columns(values):
+    return [values[:, at : at + LANES] for at in range(0, values.shape[1], LANES)]
+
+
+def encode(blocks, first=0):
+    row = lax.broadcasted_iota(I32, (LEVEL_ROWS, LANES), 0)
+    levels = jnp.zeros((LEVEL_ROWS, LANES), F32)
+    codes = []
+    for g, block in enumerate(blocks):
+        top = jnp.max(jnp.abs(block), axis=0, keepdims=True)
+        level = jnp.ceil(jnp.log2(jnp.maximum(top, 1e-30)) * PER_OCTAVE) + 1.0
+        codes.append(jnp.round(block * (jnp.exp2(level * (-1.0 / PER_OCTAVE)) * CODE_TOP)))
+        levels = jnp.where(row == first + g, level, levels)
+    return codes, levels
+
+
+def narrow(values):
+    return values.astype(I32).astype(I16)
 
 
 def decode(coded):
     rows = coded.astype(I32).astype(F32)
-    count = rows.shape[0] - CODE_ROWS
-    level = rows[count : count + 1]
-    return rows[:count] * (jnp.exp2(level * (1.0 / PER_OCTAVE)) * (1.0 / CODE_TOP))
+    count = rows.shape[0] - LEVEL_ROWS
+    scales = jnp.exp2(rows[count:] * (1.0 / PER_OCTAVE)) * (1.0 / CODE_TOP)
+    per = count // BLOCKS
+    return [rows[g * per : (g + 1) * per] * scales[g : g + 1] for g in range(BLOCKS)]
 
 
 def project(acts, gate_own, gate_sib, up_own, up_sib, down_own, down_sib, out):
     per, width = acts.shape[1], acts.shape[2] // 2
     rows = acts[...].reshape(-1, 2 * width)
     tokens, grads = rows[:, :width], rows[:, width:]
-    hid = gate_own.shape[1]
+    levels = [0.0] * NY
 
     def put(k, sums):
         for j in range(NY):
-            out[j, :, k * hid : (k + 1) * hid] = encode(sums[j * per : (j + 1) * per])
+            first = k * (sums.shape[1] // LANES)
+            codes, level = encode(columns(sums[j * per : (j + 1) * per]), first)
+            levels[j] = levels[j] + level
+            for g, code in enumerate(codes):
+                out[j, (first + g) * per : (first + g + 1) * per] = narrow(code)
 
     put(0, jnp.dot(tokens, gate_own[...], preferred_element_type=F32))
     put(1, jnp.dot(tokens, up_own[...], preferred_element_type=F32))
@@ -53,31 +72,37 @@
     put(3, jnp.dot(tokens, gate_sib[...], preferred_element_type=F32))
     put(4, jnp.dot(tokens, up_sib[...], preferred_element_type=F32))
     put(5, lax.dot_general(grads, down_sib[...], NT, preferred_element_type=F32))
+    for j in range(NY):
+        out[j, BLOCKS * per :] = narrow(levels[j])
 
 
 def add_parts(parts, coded):
-    value = decode(parts[0])
+    values = decode(parts[0])
     for j in range(1, NY):
-        value = value + decode(parts[j])
-    coded[...] = encode(value)
+        values = [a + b for a, b in zip(values, decode(parts[j]))]
+    codes, levels = encode(values)
+    coded[...] = narrow(jnp.concatenate([*codes, levels], axis=0))
 
 
 def swiglu_kernel(coded, low):
-    values = decode(coded[0]) + decode(coded[1])
-    hid = values.shape[1] // (3 * NC)
-    for k in range(NC):
-        at = 3 * k * hid
-        gate, up, hidden_grad = (values[:, at + i * hid : at + (i + 1) * hid] for i in range(3))
+    values = [a + b for a, b in zip(decode(coded[0]), decode(coded[1]))]
+    per = BLOCKS // (3 * NC)
+    for g in range(BLOCKS):
+        if (g // per) % 3:
+            continue
+        gate, up, hidden_grad = values[g], values[g + per], values[g + 2 * per]
         sigmoid = 1.0 / (1.0 + jnp.exp(-gate))
         active = gate * sigmoid
         slope = sigmoid * (1.0 + gate * (1.0 - sigmoid))
         results = (hidden_grad * up * slope, hidden_grad * active, active * up)
         for i, result in enumerate(results):
-            low[:, at + i * hid : at + (i + 1) * hid] = result.astype(BF16)
-
-
-def input_grad(low, gate_own, gate_sib, up_own, up_sib, out):
+            at = (g + i * per) * LANES
+            low[:, at : at + LANES] = result.astype(BF16)
+
+
+def input_grad(low, gate_own, gate_sib, up_own, up_sib, out, low_away):
     rows = low[...].reshape(-1, low.shape[-1])
+    low_away[...] = rows[:, low_away.shape[1] :]
     hid = gate_own.shape[1]
     total = None
     for k, weight in ((0, gate_own), (1, up_own), (3, gate_sib), (4, up_sib)):
@@ -105,9 +130,13 @@
     def tile(ref, start):
         return ref[:, pl.ds(pl.multiple_of(start, BLOCK), BLOCK)]
 
-    def pair(own, sib, left, right_own, right_sib, right):
-        first = lax.dot_general(tile(own, left), tile(right_own, right), TN, preferred_element_type=F32)
-        second = lax.dot_general(tile(sib, left), tile(right_sib, right), TN, preferred_element_type=F32)
+    def pair(own, own_at, sib, sib_at, right_own, right_own_at, right_sib, right_sib_at):
+        first = lax.dot_general(
+            tile(own, own_at), tile(right_own, right_own_at), TN, preferred_element_type=F32
+        )
+        second = lax.dot_general(
+            tile(sib, sib_at), tile(right_sib, right_sib_at), TN, preferred_element_type=F32
+        )
         return (first + second) * scale
 
     def fill(out, count, compute):
@@ -126,7 +155,8 @@
         def compute(s):
             b = ids[s]
             per = hid // BLOCK
-            return pair(act_own, act_sib, (b // per) * BLOCK, low_own, low_sib, base + (b % per) * BLOCK)
+            left, right = (b // per) * BLOCK, base + (b % per) * BLOCK
+            return pair(act_own, left, act_sib, left, low_own, right, low_sib, right)
 
         return compute
 
@@ -134,7 +164,7 @@
         b = down_ids[s]
         per = width // BLOCK
         left, right = 2 * hid + (b // per) * BLOCK, width + (b % per) * BLOCK
-        return pair(low_own, low_sib, left, act_own, act_sib, right)
+        return pair(low_own, left, low_sib, left, act_own, right, act_sib, right)
 
     fill(gate_out, counts[0], from_tokens(gate_ids, 0))
     fill(up_out, counts[1], from_tokens(up_ids, hid))
@@ -145,8 +175,8 @@
 SMEM = pl.BlockSpec(memory_space=pltpu.SMEM)
 
 
-def call(kernel, outs, *args, specs=None):
-    shapes = [jax.ShapeDtypeStruct(s, d) for s, d in outs]
+def call(kernel, outs, *args, specs=None, in_hbm=False):
+    shapes = [pltpu.HBM(s, d) if in_hbm else jax.ShapeDtypeStruct(s, d) for s, d in outs]
     single = len(shapes) == 1
     return pl.pallas_call(
         kernel,
@@ -178,19 +208,21 @@
     acts, gate_s, up_s, down_s = lax.optimization_barrier((acts, swap(gate_w), swap(up_w), swap(down_w)))
     acts = spread(acts, "row", X_GROUPS)
 
-    coded = part + CODE_ROWS
-    sums = call(project, [((NY, coded, cols), I16)], acts, gate_w, gate_s, up_w, up_s, down_w, down_s)
+    coded = BLOCKS * part + LEVEL_ROWS
+    sums = call(project, [((NY, coded, LANES), I16)], acts, gate_w, gate_s, up_w, up_s, down_w, down_s, in_hbm=True)
     sums = lax.all_to_all(sums, "col", 0, 0, axis_index_groups=Y_GROUPS)
     acts = acts.reshape(half, 2 * width)
-    code = call(add_parts, [((coded, cols), I16)], sums)
+    code = call(add_parts, [((coded, LANES), I16)], sums)
     code = lax.all_gather(code, "col", axis=0, axis_index_groups=H_GROUPS)
     low = call(swiglu_kernel, [((part, cols), BF16)], code)
     low = lax.all_gather(low, "col", axis=0, axis_index_groups=Y_GROUPS)
 
-    grad = call(input_grad, [((NX, part, width), BF16)], low, gate_w, gate_s, up_w, up_s)
+    grad, low_away = call(
+        input_grad, [((NX, part, width), BF16), ((half, cols // NC), BF16)], low, gate_w, gate_s, up_w, up_s, in_hbm=True
+    )
     grad = lax.all_to_all(grad, "row", 0, 0, axis_index_groups=X_GROUPS)
     low = low.reshape(half, cols)
-    grad, low_s, acts_s = lax.optimization_barrier((grad, swap(low[:, cols // NC :]), swap(acts)))
+    grad, low_s, acts_s = lax.optimization_barrier((grad, swap(low_away), swap(acts)))
     grad = call(add_rows, [((part, width), BF16)], grad).reshape(NZ, rows, width)
     grad = lax.all_to_all(grad, "row", 0, 0, axis_index_groups=Z_GROUPS)
     grad = call(add_rows, [((rows, width), F32)], grad)

time: 139 us -> 135 us (0.971)
  transfers between devices with their start and end apart: 9 -> 9, of which waited for: 5 -> 5; matrix products, arithmetic and copies ran while one was open for 1% -> 0% of each run, Pallas kernels for 5% -> 5%
where the time goes in v3:
time: 135 us
  blocking collectives  55.4 us (41%)
  starting transfers between devices  37.1 us (27%)
  waiting for transfers between devices  28.3 us (21%)
  Pallas kernels  9.76 us (7%)
  local copies, waits for them, and re-layouts  2.32 us (2%)
    all_gather x1, blocking collectives, body(): code = lax.all_gather(code, 'col', axis=0, axis_index_groups=H_GROUPS)  27.8 us
    all_to_all x1, blocking collectives, spread(): lax.all_to_all(jnp.broadcast_to(values[None], (count,) + values.shape), a...  14.2 us
    all_gather x1, blocking collectives, body(): low = lax.all_gather(low, 'col', axis=0, axis_index_groups=Y_GROUPS)  13.4 us
    all_to_all x1, starting transfers between devices, spread(): lax.all_to_all(jnp.broadcast_to(values[None], (count,) + values.shape), a...  12.5 us
    ppermute x5, starting transfers between devices, swap(): return lax.ppermute(v, 'row', CORE_SWAP)  10.1 us
    pallas_call x7, Pallas kernels, call(): pl.pallas_call(kernel, out_shape=shapes[0] if single else shapes, in_spec...  9.76 us
    all_to_all x1, waiting for transfers between devices, body(): sums = lax.all_to_all(sums, 'col', 0, 0, axis_index_groups=Y_GROUPS)  7.66 us
    all_to_all x1, waiting for transfers between devices, spread(): lax.all_to_all(jnp.broadcast_to(values[None], (count,) + values.shape), a...  7.52 us
  transfers between devices with their start and end apart: 9, of which 5 were waited for; matrix products, arithmetic and copies ran while one was open for 0% of the time, Pallas kernels for 5%

profile of v3, /device:TPU:2, one launch (start us, length us, event | category | flops | bytes accessed | tf_op | source)
XLA Modules:
  0.0 134.5 jit_solution(510482698770249094)
XLA Ops:
  0.6 0.0 copy-start
  0.6 0.8 pad_maximum_fusion
  1.4 0.7 broadcast_in_dim.10
  2.2 12.5 %all-to-all-start = ((bf16[8,8,2048]{2,1,0:T(8,128)(2,1)}), bf16[8,8,2048]{2,1,0:T(8,128)(2,1)S(1)}, u32[]{:S(2)}, u32[]{:S(2)}) async-start(bf16[8,8,2048]{2,1,0:T(8,128)(2,1)} %broadcast_in_dim.10), calls=%async_computation | async-start | bytes 524288 | tf_op jit(solution)/shard_map/all_to_all | solution.py:192
  14.7 0.0 copy-done
  14.7 1.9 %collective-permute-start = (bf16[1024,256]{1,0:T(8,128)(2,1)S(1)}, bf16[1024,256]{1,0:T(8,128)(2,1)S(1)}, u32[]{:S(2)}, u32[]{:S(2)}) collective-permute-start(bf16[1024,256]{1,0:T(8,128)(2,1)S(1)} %copy-done), channel_id=1, source_target_pairs={{0,1},{1,0},{2,3},{3,2},{4,5},{5,4},{6,7},{7,6},{8,9},{9,8},{10,11... | collective-permute-start | bytes 1572872 | tf_op jit(solution)/shard_map/ppermute | solution.py:205
  16.6 2.4 %collective-permute-start.1 = (bf16[1024,256]{1,0:T(8,128)(2,1)}, bf16[1024,256]{1,0:T(8,128)(2,1)S(1)}, u32[]{:S(2)}, u32[]{:S(2)}) collective-permute-start(bf16[1024,256]{1,0:T(8,128)(2,1)} %up_own.3), channel_id=1, source_target_pairs={{0,1},{1,0},{2,3},{3,2},{4,5},{5,4},{6,7},{7,6},{8,9},{9,8},{10,11... | collective-permute-start | bytes 1572872 | tf_op jit(solution)/shard_map/ppermute | solution.py:205
  19.0 1.9 %collective-permute-start.2 = (bf16[256,1024]{1,0:T(8,128)(2,1)}, bf16[256,1024]{1,0:T(8,128)(2,1)S(1)}, u32[]{:S(2)}, u32[]{:S(2)}) collective-permute-start(bf16[256,1024]{1,0:T(8,128)(2,1)} %down_own.1), channel_id=1, source_target_pairs={{0,1},{1,0},{2,3},{3,2},{4,5},{5,4},{6,7},{7,6},{8,9},{9,8},{10,11... | collective-permute-start | bytes 1572872 | tf_op jit(solution)/shard_map/ppermute | solution.py:205
  21.0 0.0 collective-permute-done.gate_sib
  21.0 0.0 collective-permute-done.1.up_sib
  21.0 0.0 copy-start.2
  21.0 2.1 %collective-permute-done.2.down_sib = bf16[256,1024]{1,0:T(8,128)(2,1)S(1)} collective-permute-done((bf16[256,1024]{1,0:T(8,128)(2,1)}, bf16[256,1024]{1,0:T(8,128)(2,1)S(1)}, u32[]{:S(2)}, u32[]{:S(2)}) %collective-permute-start.2) | collective-permute-done | bytes 524320 | tf_op jit(solution)/shard_map/ppermute | solution.py:205
  23.1 0.0 copy-start.5
  23.1 0.8 copy-done.5
  23.8 7.5 %all-to-all-done = bf16[8,8,2048]{2,1,0:T(8,128)(2,1)S(1)} async-done(((bf16[8,8,2048]{2,1,0:T(8,128)(2,1)}), bf16[8,8,2048]{2,1,0:T(8,128)(2,1)S(1)}, u32[]{:S(2)}, u32[]{:S(2)}) %all-to-all-start) | async-done | bytes 262176 | tf_op jit(solution)/shard_map/all_to_all | solution.py:192
  31.4 0.1 broadcast_in_dim.22
  31.5 0.0 copy-start.1
  31.5 0.0 copy-start.4
  31.5 0.0 copy-start.6
  31.5 14.2 %all_to_all.25.acts = bf16[4,64,2048]{2,1,0:T(8,128)(2,1)S(1)} all-to-all(bf16[4,64,2048]{2,1,0:T(8,128)(2,1)S(1)} %broadcast_in_dim.22), channel_id=1, replica_groups={{0,2,4,6},{1,3,5,7},{8,10,12,14},{9,11,13,15},{16,18,20,22},{17,19,21,2..., dimensions={0} | all-to-all | bytes 2097152 | tf_op jit(solution)/shard_map/all_to_all | solution.py:192
  45.7 0.0 copy-done.2
  45.7 0.0 copy-done.1
  45.7 0.0 copy-done.4
  45.7 0.0 copy-done.6
  45.7 2.0 %shard_map.120 = s16[4,784,128]{2,1,0:T(8,128)(2,1)} custom-call(bf16[4,64,2048]{2,1,0:T(8,128)(2,1)S(1)} %all_to_all.25.acts, bf16[1024,256]{1,0:T(8,128)(2,1)S(1)} %copy-done, bf16[1024,256]{1,0:T(8,128)(2,1)S(1)} %collective-permute-done.gate_sib, bf16[1024,256]{1,0:T(8,128)(2,1)S(1)} %copy-done.1, bf16[1024,256]{1,0:T(8,128)(2,1)S(1)} %collective-permute-done.1.up_sib, ...), custom_call_target="tpu_custom_call" | custom-call | tf_op jit(solution)/shard_map/pallas_call | solution.py:181
  47.7 4.5 %all-to-all-start.2 = ((s16[4,784,128]{2,1,0:T(8,128)(2,1)}), s16[4,784,128]{2,1,0:T(8,128)(2,1)S(1)}, u32[]{:S(2)}, u32[]{:S(2)}) async-start(s16[4,784,128]{2,1,0:T(8,128)(2,1)} %shard_map.120), calls=%async_computation.2 | async-start | bytes 1605632 | tf_op jit(solution)/shard_map/all_to_all | solution.py:213
  52.2 1.9 %collective-permute-start.4 = (bf16[256,2048]{1,0:T(8,128)(2,1)S(1)}, bf16[256,2048]{1,0:T(8,128)(2,1)}, u32[]{:S(2)}, u32[]{:S(2)}) collective-permute-start(bf16[256,2048]{1,0:T(8,128)(2,1)S(1)} %bitcast.12), channel_id=1, source_target_pairs={{0,1},{1,0},{2,3},{3,2},{4,5},{5,4},{6,7},{7,6},{8,9},{9,8},{10,11... | collective-permute-start | bytes 3145736 | tf_op jit(solution)/shard_map/ppermute | solution.py:205
  54.1 7.7 %all-to-all-done.2.parts = s16[4,784,128]{2,1,0:T(8,128)(2,1)S(1)} async-done(((s16[4,784,128]{2,1,0:T(8,128)(2,1)}), s16[4,784,128]{2,1,0:T(8,128)(2,1)S(1)}, u32[]{:S(2)}, u32[]{:S(2)}) %all-to-all-start.2) | async-done | bytes 802848 | tf_op jit(solution)/shard_map/all_to_all | solution.py:213
  61.8 0.3 shard_map.121
  62.1 27.8 %all-gather = s16[1568,128]{1,0:T(8,128)(2,1)S(1)} all-gather(s16[784,128]{1,0:T(8,128)(2,1)S(1)} %shard_map.121), channel_id=2, replica_groups={{0,64},{128,192},{256,320},{384,448},{1,65},{129,193},{257,321},{385,44..., dimensions={0}, use_global_device_ids=true | all-gather | bytes 602112 | tf_op jit(solution)/shard_map/all_gather | solution.py:216
  89.9 0.2 shard_map.122
  90.0 0.0 copy-start.3
  90.0 13.4 %all-gather.1.low_own = bf16[256,1536]{1,0:T(8,128)(2,1)S(1)} all-gather(bf16[64,1536]{1,0:T(8,128)(2,1)S(1)} %shard_map.122), channel_id=3, replica_groups={{0,128,256,384},{64,192,320,448},{1,129,257,385},{65,193,321,449},{2,13..., dimensions={0}, use_global_device_ids=true | all-gather | bytes 983040 | tf_op jit(solution)/shard_map/all_gather | solution.py:218
  103.5 0.0 copy-done.3
  103.5 1.6 %shard_map.123 = (bf16[4,64,1024]{2,1,0:T(8,128)(2,1)}, bf16[256,768]{1,0:T(8,128)(2,1)}) custom-call(bf16[4,64,1536]{2,1,0:T(8,128)(2,1)S(1)} %bitcast.14, bf16[1024,256]{1,0:T(8,128)(2,1)S(1)} %copy-done, bf16[1024,256]{1,0:T(8,128)(2,1)S(1)} %collective-permute-done.gate_sib, bf16[1024,256]{1,0:T(8,128)(2,1)S(1)} %copy-done.1, bf16[1024,256]{1,0:T(8,128)(2,1)S(1)} %copy-done.3), custom_call_target="tpu_custom_call" | custom-call | tf_op jit(solution)/shard_map/pallas_call | solution.py:181
  105.1 0.0 copy-start.11
  105.1 5.0 %all-to-all-start.3 = ((bf16[4,64,1024]{2,1,0:T(8,128)(2,1)}), bf16[4,64,1024]{2,1,0:T(8,128)(2,1)S(1)}, u32[]{:S(2)}, u32[]{:S(2)}) async-start(bf16[4,64,1024]{2,1,0:T(8,128)(2,1)} %get-tuple-element.20), calls=%async_computation.3 | async-start | bytes 1048576 | tf_op jit(solution)/shard_map/all_to_all | solution.py:223
  110.1 0.0 copy-done.11
  110.1 1.9 %collective-permute-start.3 = (bf16[256,768]{1,0:T(8,128)(2,1)S(1)}, bf16[256,768]{1,0:T(8,128)(2,1)S(1)}, u32[]{:S(2)}, u32[]{:S(2)}) collective-permute-start(bf16[256,768]{1,0:T(8,128)(2,1)S(1)} %copy-done.11), channel_id=1, source_target_pairs={{0,1},{1,0},{2,3},{3,2},{4,5},{5,4},{6,7},{7,6},{8,9},{9,8},{10,11... | collective-permute-start | bytes 1179656 | tf_op jit(solution)/shard_map/ppermute | solution.py:205
  112.0 4.7 %all-to-all-done.3.parts = bf16[4,64,1024]{2,1,0:T(8,128)(2,1)S(1)} async-done(((bf16[4,64,1024]{2,1,0:T(8,128)(2,1)}), bf16[4,64,1024]{2,1,0:T(8,128)(2,1)S(1)}, u32[]{:S(2)}, u32[]{:S(2)}) %all-to-all-start.3) | async-done | bytes 524320 | tf_op jit(solution)/shard_map/all_to_all | solution.py:223
  116.7 0.0 collective-permute-done.3.low_sib
  116.8 0.0 collective-permute-done.4.act_sib
  116.8 0.7 shard_map.124
  117.5 0.0 copy-start.10
  117.5 5.0 %all-to-all-start.4 = ((bf16[8,8,1024]{2,1,0:T(8,128)(2,1)}), bf16[8,8,1024]{2,1,0:T(8,128)(2,1)S(1)}, u32[]{:S(2)}, u32[]{:S(2)}) async-start(bf16[8,8,1024]{2,1,0:T(8,128)(2,1)} %bitcast.4), calls=%async_computation.4 | async-start | bytes 262144 | tf_op jit(solution)/shard_map/all_to_all | solution.py:227
  122.5 0.0 copy-start.7
  122.5 0.0 copy-start.8
  122.5 0.0 copy-start.9
  122.5 0.0 copy-done.10
  122.5 0.6 copy-done.7
  123.1 0.0 copy-done.8
  123.2 0.0 copy-done.9
  123.2 4.4 %shard_map.126 = (f32[8,128,128]{2,1,0:T(8,128)}, f32[8,128,128]{2,1,0:T(8,128)}, f32[8,128,128]{2,1,0:T(8,128)}) custom-call(s32[8]{0:T(128)S(1)} %bitcast.16, s32[8]{0:T(128)S(1)} %bitcast.17, s32[8]{0:T(128)S(1)} %bitcast.18, s32[3]{0:T(128)S(1)} %bitcast.19, bf16[256,2048]{1,0:T(8,128)(2,1)S(1)} %bitcast.13, ...), custom_call_target="tpu_custom_call" | custom-call | tf_op jit(solution)/shard_map/pallas_call | solution.py:181
  127.5 6.4 %all-to-all-done.4.parts = bf16[8,8,1024]{2,1,0:T(8,128)(2,1)S(1)} async-done(((bf16[8,8,1024]{2,1,0:T(8,128)(2,1)}), bf16[8,8,1024]{2,1,0:T(8,128)(2,1)S(1)}, u32[]{:S(2)}, u32[]{:S(2)}) %all-to-all-start.4) | async-done | bytes 131104 | tf_op jit(solution)/shard_map/all_to_all | solution.py:227
  133.9 0.6 shard_map.125
Async XLA Ops:
  0.6 14.1 %copy-start = (bf16[1024,256]{1,0:T(8,128)(2,1)S(1)}, bf16[1024,256]{1,0:T(8,128)(2,1)}, u32[]{:S(2)}) copy-start(bf16[1024,256]{1,0:T(8,128)(2,1)} %gate_own.3) | copy-start | bytes 1572868
  2.2 29.2 %all-to-all-start = ((bf16[8,8,2048]{2,1,0:T(8,128)(2,1)}), bf16[8,8,2048]{2,1,0:T(8,128)(2,1)S(1)}, u32[]{:S(2)}, u32[]{:S(2)}) async-start(bf16[8,8,2048]{2,1,0:T(8,128)(2,1)} %broadcast_in_dim.10), calls=%async_computation | async-start | bytes 524288 | tf_op jit(solution)/shard_map/all_to_all | solution.py:192
  14.7 6.3 %collective-permute-start = (bf16[1024,256]{1,0:T(8,128)(2,1)S(1)}, bf16[1024,256]{1,0:T(8,128)(2,1)S(1)}, u32[]{:S(2)}, u32[]{:S(2)}) collective-permute-start(bf16[1024,256]{1,0:T(8,128)(2,1)S(1)} %copy-done), channel_id=1, source_target_pairs={{0,1},{1,0},{2,3},{3,2},{4,5},{5,4},{6,7},{7,6},{8,9},{9,8},{10,11... | collective-permute-start | bytes 1572872 | tf_op jit(solution)/shard_map/ppermute | solution.py:205
  16.6 4.4 %collective-permute-start.1 = (bf16[1024,256]{1,0:T(8,128)(2,1)}, bf16[1024,256]{1,0:T(8,128)(2,1)S(1)}, u32[]{:S(2)}, u32[]{:S(2)}) collective-permute-start(bf16[1024,256]{1,0:T(8,128)(2,1)} %up_own.3), channel_id=1, source_target_pairs={{0,1},{1,0},{2,3},{3,2},{4,5},{5,4},{6,7},{7,6},{8,9},{9,8},{10,11... | collective-permute-start | bytes 1572872 | tf_op jit(solution)/shard_map/ppermute | solution.py:205
  19.0 4.0 %collective-permute-start.2 = (bf16[256,1024]{1,0:T(8,128)(2,1)}, bf16[256,1024]{1,0:T(8,128)(2,1)S(1)}, u32[]{:S(2)}, u32[]{:S(2)}) collective-permute-start(bf16[256,1024]{1,0:T(8,128)(2,1)} %down_own.1), channel_id=1, source_target_pairs={{0,1},{1,0},{2,3},{3,2},{4,5},{5,4},{6,7},{7,6},{8,9},{9,8},{10,11... | collective-permute-start | bytes 1572872 | tf_op jit(solution)/shard_map/ppermute | solution.py:205
  21.0 24.7 %copy-start.2 = (bf16[1024,256]{1,0:T(8,128)(2,1)}, bf16[1024,256]{1,0:T(8,128)(2,1)S(1)}, u32[]{:S(2)}) copy-start(bf16[1024,256]{1,0:T(8,128)(2,1)S(1)} %collective-permute-done.1.up_sib) | copy-start | bytes 1572868
  23.1 0.8 copy-start.5
  31.5 14.2 %copy-start.1 = (bf16[1024,256]{1,0:T(8,128)(2,1)S(1)}, bf16[1024,256]{1,0:T(8,128)(2,1)}, u32[]{:S(2)}) copy-start(bf16[1024,256]{1,0:T(8,128)(2,1)} %up_own.3) | copy-start | bytes 1572868
  31.5 14.2 %copy-start.4 = (bf16[256,1024]{1,0:T(8,128)(2,1)S(1)}, bf16[256,1024]{1,0:T(8,128)(2,1)}, u32[]{:S(2)}) copy-start(bf16[256,1024]{1,0:T(8,128)(2,1)} %down_own.1) | copy-start | bytes 1572868
  31.5 14.2 %copy-start.6 = (bf16[256,1024]{1,0:T(8,128)(2,1)S(1)}, bf16[256,1024]{1,0:T(8,128)(2,1)}, u32[]{:S(2)}) copy-start(bf16[256,1024]{1,0:T(8,128)(2,1)} %copy-done.5) | copy-start | bytes 1572868
  47.7 14.0 %all-to-all-start.2 = ((s16[4,784,128]{2,1,0:T(8,128)(2,1)}), s16[4,784,128]{2,1,0:T(8,128)(2,1)S(1)}, u32[]{:S(2)}, u32[]{:S(2)}) async-start(s16[4,784,128]{2,1,0:T(8,128)(2,1)} %shard_map.120), calls=%async_computation.2 | async-start | bytes 1605632 | tf_op jit(solution)/shard_map/all_to_all | solution.py:213
  52.2 64.6 %collective-permute-start.4 = (bf16[256,2048]{1,0:T(8,128)(2,1)S(1)}, bf16[256,2048]{1,0:T(8,128)(2,1)}, u32[]{:S(2)}, u32[]{:S(2)}) collective-permute-start(bf16[256,2048]{1,0:T(8,128)(2,1)S(1)} %bitcast.12), channel_id=1, source_target_pairs={{0,1},{1,0},{2,3},{3,2},{4,5},{5,4},{6,7},{7,6},{8,9},{9,8},{10,11... | collective-permute-start | bytes 3145736 | tf_op jit(solution)/shard_map/ppermute | solution.py:205
  90.0 13.5 %copy-start.3 = (bf16[1024,256]{1,0:T(8,128)(2,1)S(1)}, bf16[1024,256]{1,0:T(8,128)(2,1)}, u32[]{:S(2)}) copy-start(bf16[1024,256]{1,0:T(8,128)(2,1)} %copy-done.2) | copy-start | bytes 1572868
  105.1 5.0 %copy-start.11 = (bf16[256,768]{1,0:T(8,128)(2,1)S(1)}, bf16[256,768]{1,0:T(8,128)(2,1)}, u32[]{:S(2)}) copy-start(bf16[256,768]{1,0:T(8,128)(2,1)} %get-tuple-element.21) | copy-start | bytes 1179652
  105.1 11.7 %all-to-all-start.3 = ((bf16[4,64,1024]{2,1,0:T(8,128)(2,1)}), bf16[4,64,1024]{2,1,0:T(8,128)(2,1)S(1)}, u32[]{:S(2)}, u32[]{:S(2)}) async-start(bf16[4,64,1024]{2,1,0:T(8,128)(2,1)} %get-tuple-element.20), calls=%async_computation.3 | async-start | bytes 1048576 | tf_op jit(solution)/shard_map/all_to_all | solution.py:223
  110.1 6.6 %collective-permute-start.3 = (bf16[256,768]{1,0:T(8,128)(2,1)S(1)}, bf16[256,768]{1,0:T(8,128)(2,1)S(1)}, u32[]{:S(2)}, u32[]{:S(2)}) collective-permute-start(bf16[256,768]{1,0:T(8,128)(2,1)S(1)} %copy-done.11), channel_id=1, source_target_pairs={{0,1},{1,0},{2,3},{3,2},{4,5},{5,4},{6,7},{7,6},{8,9},{9,8},{10,11... | collective-permute-start | bytes 1179656 | tf_op jit(solution)/shard_map/ppermute | solution.py:205
  117.5 5.1 %copy-start.10 = (s32[1,1,3]{2,1,0:T(1,128)S(1)}, s32[1,1,3]{2,1,0:T(1,128)}, u32[]{:S(2)}) copy-start(s32[1,1,3]{2,1,0:T(1,128)} %param.17) | copy-start | bytes 40
  117.5 16.4 %all-to-all-start.4 = ((bf16[8,8,1024]{2,1,0:T(8,128)(2,1)}), bf16[8,8,1024]{2,1,0:T(8,128)(2,1)S(1)}, u32[]{:S(2)}, u32[]{:S(2)}) async-start(bf16[8,8,1024]{2,1,0:T(8,128)(2,1)} %bitcast.4), calls=%async_computation.4 | async-start | bytes 262144 | tf_op jit(solution)/shard_map/all_to_all | solution.py:227
  122.5 0.7 copy-start.7
  122.5 0.7 copy-start.8
  122.5 0.7 copy-start.9

commit v4 on v3

--- a/solution.py
+++ b/solution.py
@@ -17,7 +17,8 @@
 TN = (((0,), (0,)), ((), ()))
 BF16, F32, I16, I32 = jnp.bfloat16, jnp.float32, jnp.int16, jnp.int32
 
-Z_GROUPS = [[z * NX * NC + w for z in range(NZ)] for w in range(NX * NC)]
+Z_ORDER = (3, 4, 2, 5, 1, 6, 0, 7)
+Z_GROUPS = [[z * NX * NC + w for z in Z_ORDER] for w in range(NX * NC)]
 X_GROUPS = [[(z * NX + x) * NC + c for x in range(NX)] for z in range(NZ) for c in range(NC)]
 Y_GROUPS = [[y * NH + h for y in range(NY)] for h in range(NH)]
 CORE_SWAP = [(r, r ^ 1) for r in range(NZ * NX * NC)]

time: 135 us -> 128 us (0.948)
  the two profiles are of different devices: /device:TPU:2 before, /device:TPU:8 now
where the time goes in v4:
time: 128 us; the launch traced here: 127 us
  blocking collectives  54.4 us (42%)
  starting transfers between devices  38 us (30%)
  waiting for transfers between devices  20.7 us (16%)
  Pallas kernels  10 us (8%)
  local copies, waits for them, and re-layouts  2.34 us (2%)
    all_gather x1, blocking collectives, body(): code = lax.all_gather(code, 'col', axis=0, axis_index_groups=H_GROUPS)  23.8 us
    all_to_all x1, blocking collectives, spread(): lax.all_to_all(jnp.broadcast_to(values[None], (count,) + values.shape), a...  17.4 us
    all_gather x1, blocking collectives, body(): low = lax.all_gather(low, 'col', axis=0, axis_index_groups=Y_GROUPS)  13.2 us
    all_to_all x1, starting transfers between devices, spread(): lax.all_to_all(jnp.broadcast_to(values[None], (count,) + values.shape), a...  13.1 us
    ppermute x5, starting transfers between devices, swap(): return lax.ppermute(v, 'row', CORE_SWAP)  10.1 us
    pallas_call x7, Pallas kernels, call(): pl.pallas_call(kernel, out_shape=shapes[0] if single else shapes, in_spec...  10 us
    all_to_all x1, starting transfers between devices, body(): grad = lax.all_to_all(grad, 'row', 0, 0, axis_index_groups=Z_GROUPS)  6.31 us
    all_to_all x1, waiting for transfers between devices, body(): sums = lax.all_to_all(sums, 'col', 0, 0, axis_index_groups=Y_GROUPS)  6.2 us
  transfers between devices with their start and end apart: 9, of which 5 were waited for; matrix products, arithmetic and copies ran while one was open for 0% of the time, Pallas kernels for 5%

profile of v4, /device:TPU:8, one launch (start us, length us, event | category | flops | bytes accessed | tf_op | source)
XLA Modules:
  0.0 127.0 jit_solution(954065985289424029)
XLA Ops:
  0.6 0.0 copy-start
  0.6 0.8 pad_maximum_fusion
  1.4 0.7 broadcast_in_dim.10
  2.2 13.1 %all-to-all-start = ((bf16[8,8,2048]{2,1,0:T(8,128)(2,1)}), bf16[8,8,2048]{2,1,0:T(8,128)(2,1)S(1)}, u32[]{:S(2)}, u32[]{:S(2)}) async-start(bf16[8,8,2048]{2,1,0:T(8,128)(2,1)} %broadcast_in_dim.10), calls=%async_computation | async-start | bytes 524288 | tf_op jit(solution)/shard_map/all_to_all | solution.py:193
  15.2 0.0 copy-done
  15.2 1.9 %collective-permute-start = (bf16[1024,256]{1,0:T(8,128)(2,1)S(1)}, bf16[1024,256]{1,0:T(8,128)(2,1)S(1)}, u32[]{:S(2)}, u32[]{:S(2)}) collective-permute-start(bf16[1024,256]{1,0:T(8,128)(2,1)S(1)} %copy-done), channel_id=1, source_target_pairs={{0,1},{1,0},{2,3},{3,2},{4,5},{5,4},{6,7},{7,6},{8,9},{9,8},{10,11... | collective-permute-start | bytes 1572872 | tf_op jit(solution)/shard_map/ppermute | solution.py:206
  17.2 2.4 %collective-permute-start.1 = (bf16[1024,256]{1,0:T(8,128)(2,1)}, bf16[1024,256]{1,0:T(8,128)(2,1)S(1)}, u32[]{:S(2)}, u32[]{:S(2)}) collective-permute-start(bf16[1024,256]{1,0:T(8,128)(2,1)} %up_own.3), channel_id=1, source_target_pairs={{0,1},{1,0},{2,3},{3,2},{4,5},{5,4},{6,7},{7,6},{8,9},{9,8},{10,11... | collective-permute-start | bytes 1572872 | tf_op jit(solution)/shard_map/ppermute | solution.py:206
  19.6 1.9 %collective-permute-start.2 = (bf16[256,1024]{1,0:T(8,128)(2,1)}, bf16[256,1024]{1,0:T(8,128)(2,1)S(1)}, u32[]{:S(2)}, u32[]{:S(2)}) collective-permute-start(bf16[256,1024]{1,0:T(8,128)(2,1)} %down_own.1), channel_id=1, source_target_pairs={{0,1},{1,0},{2,3},{3,2},{4,5},{5,4},{6,7},{7,6},{8,9},{9,8},{10,11... | collective-permute-start | bytes 1572872 | tf_op jit(solution)/shard_map/ppermute | solution.py:206
  21.5 0.0 collective-permute-done.gate_sib
  21.5 0.0 collective-permute-done.1.up_sib
  21.5 0.0 copy-start.2
  21.5 2.1 %collective-permute-done.2.down_sib = bf16[256,1024]{1,0:T(8,128)(2,1)S(1)} collective-permute-done((bf16[256,1024]{1,0:T(8,128)(2,1)}, bf16[256,1024]{1,0:T(8,128)(2,1)S(1)}, u32[]{:S(2)}, u32[]{:S(2)}) %collective-permute-start.2) | collective-permute-done | bytes 524320 | tf_op jit(solution)/shard_map/ppermute | solution.py:206
  23.6 0.0 copy-start.5
  23.6 0.8 copy-done.5
  24.4 4.2 %all-to-all-done = bf16[8,8,2048]{2,1,0:T(8,128)(2,1)S(1)} async-done(((bf16[8,8,2048]{2,1,0:T(8,128)(2,1)}), bf16[8,8,2048]{2,1,0:T(8,128)(2,1)S(1)}, u32[]{:S(2)}, u32[]{:S(2)}) %all-to-all-start) | async-done | bytes 262176 | tf_op jit(solution)/shard_map/all_to_all | solution.py:193
  28.6 0.1 broadcast_in_dim.22
  28.8 0.0 copy-start.1
  28.8 0.0 copy-start.4
  28.8 0.0 copy-start.6
  28.8 17.4 %all_to_all.25.acts = bf16[4,64,2048]{2,1,0:T(8,128)(2,1)S(1)} all-to-all(bf16[4,64,2048]{2,1,0:T(8,128)(2,1)S(1)} %broadcast_in_dim.22), channel_id=1, replica_groups={{0,2,4,6},{1,3,5,7},{8,10,12,14},{9,11,13,15},{16,18,20,22},{17,19,21,2..., dimensions={0} | all-to-all | bytes 2097152 | tf_op jit(solution)/shard_map/all_to_all | solution.py:193
  46.2 0.0 copy-done.2
  46.2 0.0 copy-done.1
  46.2 0.0 copy-done.4
  46.2 0.0 copy-done.6
  46.2 2.0 %shard_map.120 = s16[4,784,128]{2,1,0:T(8,128)(2,1)} custom-call(bf16[4,64,2048]{2,1,0:T(8,128)(2,1)S(1)} %all_to_all.25.acts, bf16[1024,256]{1,0:T(8,128)(2,1)S(1)} %copy-done, bf16[1024,256]{1,0:T(8,128)(2,1)S(1)} %collective-permute-done.gate_sib, bf16[1024,256]{1,0:T(8,128)(2,1)S(1)} %copy-done.1, bf16[1024,256]{1,0:T(8,128)(2,1)S(1)} %collective-permute-done.1.up_sib, ...), custom_call_target="tpu_custom_call" | custom-call | tf_op jit(solution)/shard_map/pallas_call | solution.py:182
  48.2 4.9 %all-to-all-start.2 = ((s16[4,784,128]{2,1,0:T(8,128)(2,1)}), s16[4,784,128]{2,1,0:T(8,128)(2,1)S(1)}, u32[]{:S(2)}, u32[]{:S(2)}) async-start(s16[4,784,128]{2,1,0:T(8,128)(2,1)} %shard_map.120), calls=%async_computation.2 | async-start | bytes 1605632 | tf_op jit(solution)/shard_map/all_to_all | solution.py:214
  53.1 1.9 %collective-permute-start.4 = (bf16[256,2048]{1,0:T(8,128)(2,1)S(1)}, bf16[256,2048]{1,0:T(8,128)(2,1)}, u32[]{:S(2)}, u32[]{:S(2)}) collective-permute-start(bf16[256,2048]{1,0:T(8,128)(2,1)S(1)} %bitcast.12), channel_id=1, source_target_pairs={{0,1},{1,0},{2,3},{3,2},{4,5},{5,4},{6,7},{7,6},{8,9},{9,8},{10,11... | collective-permute-start | bytes 3145736 | tf_op jit(solution)/shard_map/ppermute | solution.py:206
  55.0 6.2 %all-to-all-done.2.parts = s16[4,784,128]{2,1,0:T(8,128)(2,1)S(1)} async-done(((s16[4,784,128]{2,1,0:T(8,128)(2,1)}), s16[4,784,128]{2,1,0:T(8,128)(2,1)S(1)}, u32[]{:S(2)}, u32[]{:S(2)}) %all-to-all-start.2) | async-done | bytes 802848 | tf_op jit(solution)/shard_map/all_to_all | solution.py:214
  61.2 0.3 shard_map.121
  61.5 23.8 %all-gather = s16[1568,128]{1,0:T(8,128)(2,1)S(1)} all-gather(s16[784,128]{1,0:T(8,128)(2,1)S(1)} %shard_map.121), channel_id=2, replica_groups={{0,64},{128,192},{256,320},{384,448},{1,65},{129,193},{257,321},{385,44..., dimensions={0}, use_global_device_ids=true | all-gather | bytes 602112 | tf_op jit(solution)/shard_map/all_gather | solution.py:217
  85.3 0.2 shard_map.122
  85.5 0.0 copy-start.3
  85.5 13.2 %all-gather.1.low_own = bf16[256,1536]{1,0:T(8,128)(2,1)S(1)} all-gather(bf16[64,1536]{1,0:T(8,128)(2,1)S(1)} %shard_map.122), channel_id=3, replica_groups={{0,128,256,384},{64,192,320,448},{1,129,257,385},{65,193,321,449},{2,13..., dimensions={0}, use_global_device_ids=true | all-gather | bytes 983040 | tf_op jit(solution)/shard_map/all_gather | solution.py:219
  98.7 0.0 copy-done.3
  98.7 1.6 %shard_map.123 = (bf16[4,64,1024]{2,1,0:T(8,128)(2,1)}, bf16[256,768]{1,0:T(8,128)(2,1)}) custom-call(bf16[4,64,1536]{2,1,0:T(8,128)(2,1)S(1)} %bitcast.14, bf16[1024,256]{1,0:T(8,128)(2,1)S(1)} %copy-done, bf16[1024,256]{1,0:T(8,128)(2,1)S(1)} %collective-permute-done.gate_sib, bf16[1024,256]{1,0:T(8,128)(2,1)S(1)} %copy-done.1, bf16[1024,256]{1,0:T(8,128)(2,1)S(1)} %copy-done.3), custom_call_target="tpu_custom_call" | custom-call | tf_op jit(solution)/shard_map/pallas_call | solution.py:182
  100.3 0.0 copy-start.11
  100.3 3.6 %all-to-all-start.3 = ((bf16[4,64,1024]{2,1,0:T(8,128)(2,1)}), bf16[4,64,1024]{2,1,0:T(8,128)(2,1)S(1)}, u32[]{:S(2)}, u32[]{:S(2)}) async-start(bf16[4,64,1024]{2,1,0:T(8,128)(2,1)} %get-tuple-element.20), calls=%async_computation.3 | async-start | bytes 1048576 | tf_op jit(solution)/shard_map/all_to_all | solution.py:224
  103.9 0.0 copy-done.11
  103.9 1.9 %collective-permute-start.3 = (bf16[256,768]{1,0:T(8,128)(2,1)S(1)}, bf16[256,768]{1,0:T(8,128)(2,1)S(1)}, u32[]{:S(2)}, u32[]{:S(2)}) collective-permute-start(bf16[256,768]{1,0:T(8,128)(2,1)S(1)} %copy-done.11), channel_id=1, source_target_pairs={{0,1},{1,0},{2,3},{3,2},{4,5},{5,4},{6,7},{7,6},{8,9},{9,8},{10,11... | collective-permute-start | bytes 1179656 | tf_op jit(solution)/shard_map/ppermute | solution.py:206
  105.9 6.1 %all-to-all-done.3.parts = bf16[4,64,1024]{2,1,0:T(8,128)(2,1)S(1)} async-done(((bf16[4,64,1024]{2,1,0:T(8,128)(2,1)}), bf16[4,64,1024]{2,1,0:T(8,128)(2,1)S(1)}, u32[]{:S(2)}, u32[]{:S(2)}) %all-to-all-start.3) | async-done | bytes 524320 | tf_op jit(solution)/shard_map/all_to_all | solution.py:224
  112.0 0.0 collective-permute-done.3.low_sib
  112.0 0.0 collective-permute-done.4.act_sib
  112.0 0.7 shard_map.124
  112.7 0.0 copy-start.10
  112.7 6.3 %all-to-all-start.4 = ((bf16[8,8,1024]{2,1,0:T(8,128)(2,1)}), bf16[8,8,1024]{2,1,0:T(8,128)(2,1)S(1)}, u32[]{:S(2)}, u32[]{:S(2)}) async-start(bf16[8,8,1024]{2,1,0:T(8,128)(2,1)} %bitcast.4), calls=%async_computation.4 | async-start | bytes 262144 | tf_op jit(solution)/shard_map/all_to_all | solution.py:228
  119.0 0.0 copy-start.7
  119.0 0.0 copy-start.8
  119.0 0.0 copy-start.9
  119.0 0.0 copy-done.10
  119.0 0.6 copy-done.7
  119.7 0.0 copy-done.8
  119.7 0.0 copy-done.9
  119.7 4.6 %shard_map.126 = (f32[8,128,128]{2,1,0:T(8,128)}, f32[8,128,128]{2,1,0:T(8,128)}, f32[8,128,128]{2,1,0:T(8,128)}) custom-call(s32[8]{0:T(128)S(1)} %bitcast.16, s32[8]{0:T(128)S(1)} %bitcast.17, s32[8]{0:T(128)S(1)} %bitcast.18, s32[3]{0:T(128)S(1)} %bitcast.19, bf16[256,2048]{1,0:T(8,128)(2,1)S(1)} %bitcast.13, ...), custom_call_target="tpu_custom_call" | custom-call | tf_op jit(solution)/shard_map/pallas_call | solution.py:182
  124.3 2.1 %all-to-all-done.4.parts = bf16[8,8,1024]{2,1,0:T(8,128)(2,1)S(1)} async-done(((bf16[8,8,1024]{2,1,0:T(8,128)(2,1)}), bf16[8,8,1024]{2,1,0:T(8,128)(2,1)S(1)}, u32[]{:S(2)}, u32[]{:S(2)}) %all-to-all-start.4) | async-done | bytes 131104 | tf_op jit(solution)/shard_map/all_to_all | solution.py:228
  126.4 0.6 shard_map.125
Async XLA Ops:
  0.6 14.6 %copy-start = (bf16[1024,256]{1,0:T(8,128)(2,1)S(1)}, bf16[1024,256]{1,0:T(8,128)(2,1)}, u32[]{:S(2)}) copy-start(bf16[1024,256]{1,0:T(8,128)(2,1)} %gate_own.3) | copy-start | bytes 1572868
  2.2 26.5 %all-to-all-start = ((bf16[8,8,2048]{2,1,0:T(8,128)(2,1)}), bf16[8,8,2048]{2,1,0:T(8,128)(2,1)S(1)}, u32[]{:S(2)}, u32[]{:S(2)}) async-start(bf16[8,8,2048]{2,1,0:T(8,128)(2,1)} %broadcast_in_dim.10), calls=%async_computation | async-start | bytes 524288 | tf_op jit(solution)/shard_map/all_to_all | solution.py:193
  15.2 6.3 %collective-permute-start = (bf16[1024,256]{1,0:T(8,128)(2,1)S(1)}, bf16[1024,256]{1,0:T(8,128)(2,1)S(1)}, u32[]{:S(2)}, u32[]{:S(2)}) collective-permute-start(bf16[1024,256]{1,0:T(8,128)(2,1)S(1)} %copy-done), channel_id=1, source_target_pairs={{0,1},{1,0},{2,3},{3,2},{4,5},{5,4},{6,7},{7,6},{8,9},{9,8},{10,11... | collective-permute-start | bytes 1572872 | tf_op jit(solution)/shard_map/ppermute | solution.py:206
  17.2 4.4 %collective-permute-start.1 = (bf16[1024,256]{1,0:T(8,128)(2,1)}, bf16[1024,256]{1,0:T(8,128)(2,1)S(1)}, u32[]{:S(2)}, u32[]{:S(2)}) collective-permute-start(bf16[1024,256]{1,0:T(8,128)(2,1)} %up_own.3), channel_id=1, source_target_pairs={{0,1},{1,0},{2,3},{3,2},{4,5},{5,4},{6,7},{7,6},{8,9},{9,8},{10,11... | collective-permute-start | bytes 1572872 | tf_op jit(solution)/shard_map/ppermute | solution.py:206
  19.6 4.0 %collective-permute-start.2 = (bf16[256,1024]{1,0:T(8,128)(2,1)}, bf16[256,1024]{1,0:T(8,128)(2,1)S(1)}, u32[]{:S(2)}, u32[]{:S(2)}) collective-permute-start(bf16[256,1024]{1,0:T(8,128)(2,1)} %down_own.1), channel_id=1, source_target_pairs={{0,1},{1,0},{2,3},{3,2},{4,5},{5,4},{6,7},{7,6},{8,9},{9,8},{10,11... | collective-permute-start | bytes 1572872 | tf_op jit(solution)/shard_map/ppermute | solution.py:206
  21.5 24.7 %copy-start.2 = (bf16[1024,256]{1,0:T(8,128)(2,1)}, bf16[1024,256]{1,0:T(8,128)(2,1)S(1)}, u32[]{:S(2)}) copy-start(bf16[1024,256]{1,0:T(8,128)(2,1)S(1)} %collective-permute-done.1.up_sib) | copy-start | bytes 1572868
  23.6 0.8 copy-start.5
  28.8 17.4 %copy-start.1 = (bf16[1024,256]{1,0:T(8,128)(2,1)S(1)}, bf16[1024,256]{1,0:T(8,128)(2,1)}, u32[]{:S(2)}) copy-start(bf16[1024,256]{1,0:T(8,128)(2,1)} %up_own.3) | copy-start | bytes 1572868
  28.8 17.4 %copy-start.4 = (bf16[256,1024]{1,0:T(8,128)(2,1)S(1)}, bf16[256,1024]{1,0:T(8,128)(2,1)}, u32[]{:S(2)}) copy-start(bf16[256,1024]{1,0:T(8,128)(2,1)} %down_own.1) | copy-start | bytes 1572868
  28.8 17.4 %copy-start.6 = (bf16[256,1024]{1,0:T(8,128)(2,1)S(1)}, bf16[256,1024]{1,0:T(8,128)(2,1)}, u32[]{:S(2)}) copy-start(bf16[256,1024]{1,0:T(8,128)(2,1)} %copy-done.5) | copy-start | bytes 1572868
  48.2 13.0 %all-to-all-start.2 = ((s16[4,784,128]{2,1,0:T(8,128)(2,1)}), s16[4,784,128]{2,1,0:T(8,128)(2,1)S(1)}, u32[]{:S(2)}, u32[]{:S(2)}) async-start(s16[4,784,128]{2,1,0:T(8,128)(2,1)} %shard_map.120), calls=%async_computation.2 | async-start | bytes 1605632 | tf_op jit(solution)/shard_map/all_to_all | solution.py:214
  53.1 58.9 %collective-permute-start.4 = (bf16[256,2048]{1,0:T(8,128)(2,1)S(1)}, bf16[256,2048]{1,0:T(8,128)(2,1)}, u32[]{:S(2)}, u32[]{:S(2)}) collective-permute-start(bf16[256,2048]{1,0:T(8,128)(2,1)S(1)} %bitcast.12), channel_id=1, source_target_pairs={{0,1},{1,0},{2,3},{3,2},{4,5},{5,4},{6,7},{7,6},{8,9},{9,8},{10,11... | collective-permute-start | bytes 3145736 | tf_op jit(solution)/shard_map/ppermute | solution.py:206
  85.5 13.2 %copy-start.3 = (bf16[1024,256]{1,0:T(8,128)(2,1)S(1)}, bf16[1024,256]{1,0:T(8,128)(2,1)}, u32[]{:S(2)}) copy-start(bf16[1024,256]{1,0:T(8,128)(2,1)} %copy-done.2) | copy-start | bytes 1572868
  100.3 3.6 %copy-start.11 = (bf16[256,768]{1,0:T(8,128)(2,1)S(1)}, bf16[256,768]{1,0:T(8,128)(2,1)}, u32[]{:S(2)}) copy-start(bf16[256,768]{1,0:T(8,128)(2,1)} %get-tuple-element.21) | copy-start | bytes 1179652
  100.3 11.7 %all-to-all-start.3 = ((bf16[4,64,1024]{2,1,0:T(8,128)(2,1)}), bf16[4,64,1024]{2,1,0:T(8,128)(2,1)S(1)}, u32[]{:S(2)}, u32[]{:S(2)}) async-start(bf16[4,64,1024]{2,1,0:T(8,128)(2,1)} %get-tuple-element.20), calls=%async_computation.3 | async-start | bytes 1048576 | tf_op jit(solution)/shard_map/all_to_all | solution.py:224
  103.9 8.0 %collective-permute-start.3 = (bf16[256,768]{1,0:T(8,128)(2,1)S(1)}, bf16[256,768]{1,0:T(8,128)(2,1)S(1)}, u32[]{:S(2)}, u32[]{:S(2)}) collective-permute-start(bf16[256,768]{1,0:T(8,128)(2,1)S(1)} %copy-done.11), channel_id=1, source_target_pairs={{0,1},{1,0},{2,3},{3,2},{4,5},{5,4},{6,7},{7,6},{8,9},{9,8},{10,11... | collective-permute-start | bytes 1179656 | tf_op jit(solution)/shard_map/ppermute | solution.py:206
  112.7 6.3 %copy-start.10 = (s32[1,1,3]{2,1,0:T(1,128)S(1)}, s32[1,1,3]{2,1,0:T(1,128)}, u32[]{:S(2)}) copy-start(s32[1,1,3]{2,1,0:T(1,128)} %param.17) | copy-start | bytes 40
  112.7 13.7 %all-to-all-start.4 = ((bf16[8,8,1024]{2,1,0:T(8,128)(2,1)}), bf16[8,8,1024]{2,1,0:T(8,128)(2,1)S(1)}, u32[]{:S(2)}, u32[]{:S(2)}) async-start(bf16[8,8,1024]{2,1,0:T(8,128)(2,1)} %bitcast.4), calls=%async_computation.4 | async-start | bytes 262144 | tf_op jit(solution)/shard_map/all_to_all | solution.py:228
  119.0 0.7 copy-start.7
  119.0 0.7 copy-start.8
  119.0 0.7 copy-start.9

commit v5 on v4

--- a/solution.py
+++ b/solution.py
@@ -17,7 +17,7 @@
 TN = (((0,), (0,)), ((), ()))
 BF16, F32, I16, I32 = jnp.bfloat16, jnp.float32, jnp.int16, jnp.int32
 
-Z_ORDER = (3, 4, 2, 5, 1, 6, 0, 7)
+Z_ORDER = (4, 3, 5, 2, 6, 1, 7, 0)
 Z_GROUPS = [[z * NX * NC + w for z in Z_ORDER] for w in range(NX * NC)]
 X_GROUPS = [[(z * NX + x) * NC + c for x in range(NX)] for z in range(NZ) for c in range(NC)]
 Y_GROUPS = [[y * NH + h for y in range(NY)] for h in range(NH)]

time: 128 us -> 126 us (0.984)
  starting transfers between devices: 38 us -> 47.6 us
  blocking collectives: 54.4 us -> 45.4 us
  waiting for transfers between devices: 20.7 us -> 17.2 us
  Pallas kernels: 10 us -> 11.5 us
    all_to_all x1, starting transfers between devices: 6.31 us -> 15.9 us  [body(): grad = lax.all_to_all(grad, 'row', 0, 0, axis_index_groups=Z_GROUPS)]
    all_gather x1, blocking collectives: 23.8 us -> 15.3 us  [body(): code = lax.all_gather(code, 'col', axis=0, axis_index_groups=H_GROUPS)]
    all_to_all x1, waiting for transfers between devices: 2.1 us -> 0.01 us  [body(): grad = lax.all_to_all(grad, 'row', 0, 0, axis_index_groups=Z_GROUPS)]
    pallas_call x7, Pallas kernels: 10 us -> 11.5 us  [call(): pl.pallas_call(kernel, out_shape=shapes[0] if single else shapes, in_spec...]
    all_to_all x1, waiting for transfers between devices: 4.24 us -> 2.82 us  [spread(): lax.all_to_all(jnp.broadcast_to(values[None], (count,) + values.shape), a...]
  transfers between devices with their start and end apart: 9 -> 9, of which waited for: 5 -> 4; matrix products, arithmetic and copies ran while one was open for 0% -> 0% of each run, Pallas kernels for 5% -> 6%
where the time goes in v5:
time: 126 us
  starting transfers between devices  47.6 us (38%)
  blocking collectives  45.4 us (36%)
  waiting for transfers between devices  17.2 us (14%)
  Pallas kernels  11.5 us (9%)
  local copies, waits for them, and re-layouts  2.34 us (2%)
    all_to_all x1, blocking collectives, spread(): lax.all_to_all(jnp.broadcast_to(values[None], (count,) + values.shape), a...  16.8 us
    all_to_all x1, starting transfers between devices, body(): grad = lax.all_to_all(grad, 'row', 0, 0, axis_index_groups=Z_GROUPS)  15.9 us
    all_gather x1, blocking collectives, body(): code = lax.all_gather(code, 'col', axis=0, axis_index_groups=H_GROUPS)  15.3 us
    all_gather x1, blocking collectives, body(): low = lax.all_gather(low, 'col', axis=0, axis_index_groups=Y_GROUPS)  13.3 us
    all_to_all x1, starting transfers between devices, spread(): lax.all_to_all(jnp.broadcast_to(values[None], (count,) + values.shape), a...  13.1 us
    pallas_call x7, Pallas kernels, call(): pl.pallas_call(kernel, out_shape=shapes[0] if single else shapes, in_spec...  11.5 us
    ppermute x5, starting transfers between devices, swap(): return lax.ppermute(v, 'row', CORE_SWAP)  10.1 us
    all_to_all x1, waiting for transfers between devices, body(): sums = lax.all_to_all(sums, 'col', 0, 0, axis_index_groups=Y_GROUPS)  6.2 us
  transfers between devices with their start and end apart: 9, of which 4 were waited for; matrix products, arithmetic and copies ran while one was open for 0% of the time, Pallas kernels for 6%

profile of v5, /device:TPU:8, one launch (start us, length us, event | category | flops | bytes accessed | tf_op | source)
XLA Modules:
  0.0 125.6 jit_solution(11993724138764804156)
XLA Ops:
  0.6 0.0 copy-start
  0.6 0.8 pad_maximum_fusion
  1.4 0.7 broadcast_in_dim.10
  2.2 13.1 %all-to-all-start = ((bf16[8,8,2048]{2,1,0:T(8,128)(2,1)}), bf16[8,8,2048]{2,1,0:T(8,128)(2,1)S(1)}, u32[]{:S(2)}, u32[]{:S(2)}) async-start(bf16[8,8,2048]{2,1,0:T(8,128)(2,1)} %broadcast_in_dim.10), calls=%async_computation | async-start | bytes 524288 | tf_op jit(solution)/shard_map/all_to_all | solution.py:193
  15.2 0.0 copy-done
  15.2 1.9 %collective-permute-start = (bf16[1024,256]{1,0:T(8,128)(2,1)S(1)}, bf16[1024,256]{1,0:T(8,128)(2,1)S(1)}, u32[]{:S(2)}, u32[]{:S(2)}) collective-permute-start(bf16[1024,256]{1,0:T(8,128)(2,1)S(1)} %copy-done), channel_id=1, source_target_pairs={{0,1},{1,0},{2,3},{3,2},{4,5},{5,4},{6,7},{7,6},{8,9},{9,8},{10,11... | collective-permute-start | bytes 1572872 | tf_op jit(solution)/shard_map/ppermute | solution.py:206
  17.2 2.4 %collective-permute-start.1 = (bf16[1024,256]{1,0:T(8,128)(2,1)}, bf16[1024,256]{1,0:T(8,128)(2,1)S(1)}, u32[]{:S(2)}, u32[]{:S(2)}) collective-permute-start(bf16[1024,256]{1,0:T(8,128)(2,1)} %up_own.3), channel_id=1, source_target_pairs={{0,1},{1,0},{2,3},{3,2},{4,5},{5,4},{6,7},{7,6},{8,9},{9,8},{10,11... | collective-permute-start | bytes 1572872 | tf_op jit(solution)/shard_map/ppermute | solution.py:206
  19.6 1.9 %collective-permute-start.2 = (bf16[256,1024]{1,0:T(8,128)(2,1)}, bf16[256,1024]{1,0:T(8,128)(2,1)S(1)}, u32[]{:S(2)}, u32[]{:S(2)}) collective-permute-start(bf16[256,1024]{1,0:T(8,128)(2,1)} %down_own.1), channel_id=1, source_target_pairs={{0,1},{1,0},{2,3},{3,2},{4,5},{5,4},{6,7},{7,6},{8,9},{9,8},{10,11... | collective-permute-start | bytes 1572872 | tf_op jit(solution)/shard_map/ppermute | solution.py:206
  21.5 0.0 collective-permute-done.gate_sib
  21.5 0.0 collective-permute-done.1.up_sib
  21.5 0.0 copy-start.2
  21.5 2.1 %collective-permute-done.2.down_sib = bf16[256,1024]{1,0:T(8,128)(2,1)S(1)} collective-permute-done((bf16[256,1024]{1,0:T(8,128)(2,1)}, bf16[256,1024]{1,0:T(8,128)(2,1)S(1)}, u32[]{:S(2)}, u32[]{:S(2)}) %collective-permute-start.2) | collective-permute-done | bytes 524320 | tf_op jit(solution)/shard_map/ppermute | solution.py:206
  23.6 0.0 copy-start.5
  23.6 0.8 copy-done.5
  24.4 2.8 %all-to-all-done = bf16[8,8,2048]{2,1,0:T(8,128)(2,1)S(1)} async-done(((bf16[8,8,2048]{2,1,0:T(8,128)(2,1)}), bf16[8,8,2048]{2,1,0:T(8,128)(2,1)S(1)}, u32[]{:S(2)}, u32[]{:S(2)}) %all-to-all-start) | async-done | bytes 262176 | tf_op jit(solution)/shard_map/all_to_all | solution.py:193
  27.2 0.1 broadcast_in_dim.22
  27.3 0.0 copy-start.1
  27.3 0.0 copy-start.4
  27.4 0.0 copy-start.6
  27.4 16.8 %all_to_all.25.acts = bf16[4,64,2048]{2,1,0:T(8,128)(2,1)S(1)} all-to-all(bf16[4,64,2048]{2,1,0:T(8,128)(2,1)S(1)} %broadcast_in_dim.22), channel_id=1, replica_groups={{0,2,4,6},{1,3,5,7},{8,10,12,14},{9,11,13,15},{16,18,20,22},{17,19,21,2..., dimensions={0} | all-to-all | bytes 2097152 | tf_op jit(solution)/shard_map/all_to_all | solution.py:193
  44.2 0.0 copy-done.2
  44.2 0.0 copy-done.1
  44.2 0.0 copy-done.4
  44.2 0.0 copy-done.6
  44.2 2.0 %shard_map.120 = s16[4,784,128]{2,1,0:T(8,128)(2,1)} custom-call(bf16[4,64,2048]{2,1,0:T(8,128)(2,1)S(1)} %all_to_all.25.acts, bf16[1024,256]{1,0:T(8,128)(2,1)S(1)} %copy-done, bf16[1024,256]{1,0:T(8,128)(2,1)S(1)} %collective-permute-done.gate_sib, bf16[1024,256]{1,0:T(8,128)(2,1)S(1)} %copy-done.1, bf16[1024,256]{1,0:T(8,128)(2,1)S(1)} %collective-permute-done.1.up_sib, ...), custom_call_target="tpu_custom_call" | custom-call | tf_op jit(solution)/shard_map/pallas_call | solution.py:182
  46.2 4.9 %all-to-all-start.2 = ((s16[4,784,128]{2,1,0:T(8,128)(2,1)}), s16[4,784,128]{2,1,0:T(8,128)(2,1)S(1)}, u32[]{:S(2)}, u32[]{:S(2)}) async-start(s16[4,784,128]{2,1,0:T(8,128)(2,1)} %shard_map.120), calls=%async_computation.2 | async-start | bytes 1605632 | tf_op jit(solution)/shard_map/all_to_all | solution.py:214
  51.1 1.9 %collective-permute-start.4 = (bf16[256,2048]{1,0:T(8,128)(2,1)S(1)}, bf16[256,2048]{1,0:T(8,128)(2,1)}, u32[]{:S(2)}, u32[]{:S(2)}) collective-permute-start(bf16[256,2048]{1,0:T(8,128)(2,1)S(1)} %bitcast.12), channel_id=1, source_target_pairs={{0,1},{1,0},{2,3},{3,2},{4,5},{5,4},{6,7},{7,6},{8,9},{9,8},{10,11... | collective-permute-start | bytes 3145736 | tf_op jit(solution)/shard_map/ppermute | solution.py:206
  53.0 6.2 %all-to-all-done.2.parts = s16[4,784,128]{2,1,0:T(8,128)(2,1)S(1)} async-done(((s16[4,784,128]{2,1,0:T(8,128)(2,1)}), s16[4,784,128]{2,1,0:T(8,128)(2,1)S(1)}, u32[]{:S(2)}, u32[]{:S(2)}) %all-to-all-start.2) | async-done | bytes 802848 | tf_op jit(solution)/shard_map/all_to_all | solution.py:214
  59.2 0.3 shard_map.121
  59.5 15.3 %all-gather = s16[1568,128]{1,0:T(8,128)(2,1)S(1)} all-gather(s16[784,128]{1,0:T(8,128)(2,1)S(1)} %shard_map.121), channel_id=2, replica_groups={{0,64},{128,192},{256,320},{384,448},{1,65},{129,193},{257,321},{385,44..., dimensions={0}, use_global_device_ids=true | all-gather | bytes 602112 | tf_op jit(solution)/shard_map/all_gather | solution.py:217
  74.8 0.2 shard_map.122
  75.0 0.0 copy-start.3
  75.0 13.3 %all-gather.1.low_own = bf16[256,1536]{1,0:T(8,128)(2,1)S(1)} all-gather(bf16[64,1536]{1,0:T(8,128)(2,1)S(1)} %shard_map.122), channel_id=3, replica_groups={{0,128,256,384},{64,192,320,448},{1,129,257,385},{65,193,321,449},{2,13..., dimensions={0}, use_global_device_ids=true | all-gather | bytes 983040 | tf_op jit(solution)/shard_map/all_gather | solution.py:219
  88.3 0.0 copy-done.3
  88.3 1.6 %shard_map.123 = (bf16[4,64,1024]{2,1,0:T(8,128)(2,1)}, bf16[256,768]{1,0:T(8,128)(2,1)}) custom-call(bf16[4,64,1536]{2,1,0:T(8,128)(2,1)S(1)} %bitcast.14, bf16[1024,256]{1,0:T(8,128)(2,1)S(1)} %copy-done, bf16[1024,256]{1,0:T(8,128)(2,1)S(1)} %collective-permute-done.gate_sib, bf16[1024,256]{1,0:T(8,128)(2,1)S(1)} %copy-done.1, bf16[1024,256]{1,0:T(8,128)(2,1)S(1)} %copy-done.3), custom_call_target="tpu_custom_call" | custom-call | tf_op jit(solution)/shard_map/pallas_call | solution.py:182
  89.9 0.0 copy-start.11
  89.9 3.6 %all-to-all-start.3 = ((bf16[4,64,1024]{2,1,0:T(8,128)(2,1)}), bf16[4,64,1024]{2,1,0:T(8,128)(2,1)S(1)}, u32[]{:S(2)}, u32[]{:S(2)}) async-start(bf16[4,64,1024]{2,1,0:T(8,128)(2,1)} %get-tuple-element.20), calls=%async_computation.3 | async-start | bytes 1048576 | tf_op jit(solution)/shard_map/all_to_all | solution.py:224
  93.5 0.0 copy-done.11
  93.5 1.9 %collective-permute-start.3 = (bf16[256,768]{1,0:T(8,128)(2,1)S(1)}, bf16[256,768]{1,0:T(8,128)(2,1)S(1)}, u32[]{:S(2)}, u32[]{:S(2)}) collective-permute-start(bf16[256,768]{1,0:T(8,128)(2,1)S(1)} %copy-done.11), channel_id=1, source_target_pairs={{0,1},{1,0},{2,3},{3,2},{4,5},{5,4},{6,7},{7,6},{8,9},{9,8},{10,11... | collective-permute-start | bytes 1179656 | tf_op jit(solution)/shard_map/ppermute | solution.py:206
  95.5 6.1 %all-to-all-done.3.parts = bf16[4,64,1024]{2,1,0:T(8,128)(2,1)S(1)} async-done(((bf16[4,64,1024]{2,1,0:T(8,128)(2,1)}), bf16[4,64,1024]{2,1,0:T(8,128)(2,1)S(1)}, u32[]{:S(2)}, u32[]{:S(2)}) %all-to-all-start.3) | async-done | bytes 524320 | tf_op jit(solution)/shard_map/all_to_all | solution.py:224
  101.6 0.0 collective-permute-done.3.low_sib
  101.6 0.0 collective-permute-done.4.act_sib
  101.6 0.7 shard_map.124
  102.3 0.0 copy-start.10
  102.3 15.9 %all-to-all-start.4 = ((bf16[8,8,1024]{2,1,0:T(8,128)(2,1)}), bf16[8,8,1024]{2,1,0:T(8,128)(2,1)S(1)}, u32[]{:S(2)}, u32[]{:S(2)}) async-start(bf16[8,8,1024]{2,1,0:T(8,128)(2,1)} %bitcast.4), calls=%async_computation.4 | async-start | bytes 262144 | tf_op jit(solution)/shard_map/all_to_all | solution.py:228
  118.2 0.0 copy-start.7
  118.2 0.0 copy-start.8
  118.2 0.0 copy-start.9
  118.2 0.0 copy-done.10
  118.2 0.6 copy-done.7
  118.9 0.0 copy-done.8
  118.9 0.0 copy-done.9
  118.9 6.1 %shard_map.126 = (f32[8,128,128]{2,1,0:T(8,128)}, f32[8,128,128]{2,1,0:T(8,128)}, f32[8,128,128]{2,1,0:T(8,128)}) custom-call(s32[8]{0:T(128)S(1)} %bitcast.16, s32[8]{0:T(128)S(1)} %bitcast.17, s32[8]{0:T(128)S(1)} %bitcast.18, s32[3]{0:T(128)S(1)} %bitcast.19, bf16[256,2048]{1,0:T(8,128)(2,1)S(1)} %bitcast.13, ...), custom_call_target="tpu_custom_call" | custom-call | tf_op jit(solution)/shard_map/pallas_call | solution.py:182
  125.0 0.0 all-to-all-done.4.parts
  125.0 0.6 shard_map.125
Async XLA Ops:
  0.6 14.6 %copy-start = (bf16[1024,256]{1,0:T(8,128)(2,1)S(1)}, bf16[1024,256]{1,0:T(8,128)(2,1)}, u32[]{:S(2)}) copy-start(bf16[1024,256]{1,0:T(8,128)(2,1)} %gate_own.3) | copy-start | bytes 1572868
  2.2 25.1 %all-to-all-start = ((bf16[8,8,2048]{2,1,0:T(8,128)(2,1)}), bf16[8,8,2048]{2,1,0:T(8,128)(2,1)S(1)}, u32[]{:S(2)}, u32[]{:S(2)}) async-start(bf16[8,8,2048]{2,1,0:T(8,128)(2,1)} %broadcast_in_dim.10), calls=%async_computation | async-start | bytes 524288 | tf_op jit(solution)/shard_map/all_to_all | solution.py:193
  15.2 6.3 %collective-permute-start = (bf16[1024,256]{1,0:T(8,128)(2,1)S(1)}, bf16[1024,256]{1,0:T(8,128)(2,1)S(1)}, u32[]{:S(2)}, u32[]{:S(2)}) collective-permute-start(bf16[1024,256]{1,0:T(8,128)(2,1)S(1)} %copy-done), channel_id=1, source_target_pairs={{0,1},{1,0},{2,3},{3,2},{4,5},{5,4},{6,7},{7,6},{8,9},{9,8},{10,11... | collective-permute-start | bytes 1572872 | tf_op jit(solution)/shard_map/ppermute | solution.py:206
  17.2 4.4 %collective-permute-start.1 = (bf16[1024,256]{1,0:T(8,128)(2,1)}, bf16[1024,256]{1,0:T(8,128)(2,1)S(1)}, u32[]{:S(2)}, u32[]{:S(2)}) collective-permute-start(bf16[1024,256]{1,0:T(8,128)(2,1)} %up_own.3), channel_id=1, source_target_pairs={{0,1},{1,0},{2,3},{3,2},{4,5},{5,4},{6,7},{7,6},{8,9},{9,8},{10,11... | collective-permute-start | bytes 1572872 | tf_op jit(solution)/shard_map/ppermute | solution.py:206
  19.6 4.0 %collective-permute-start.2 = (bf16[256,1024]{1,0:T(8,128)(2,1)}, bf16[256,1024]{1,0:T(8,128)(2,1)S(1)}, u32[]{:S(2)}, u32[]{:S(2)}) collective-permute-start(bf16[256,1024]{1,0:T(8,128)(2,1)} %down_own.1), channel_id=1, source_target_pairs={{0,1},{1,0},{2,3},{3,2},{4,5},{5,4},{6,7},{7,6},{8,9},{9,8},{10,11... | collective-permute-start | bytes 1572872 | tf_op jit(solution)/shard_map/ppermute | solution.py:206
  21.5 22.6 %copy-start.2 = (bf16[1024,256]{1,0:T(8,128)(2,1)}, bf16[1024,256]{1,0:T(8,128)(2,1)S(1)}, u32[]{:S(2)}) copy-start(bf16[1024,256]{1,0:T(8,128)(2,1)S(1)} %collective-permute-done.1.up_sib) | copy-start | bytes 1572868
  23.6 0.8 copy-start.5
  27.3 16.8 %copy-start.1 = (bf16[1024,256]{1,0:T(8,128)(2,1)S(1)}, bf16[1024,256]{1,0:T(8,128)(2,1)}, u32[]{:S(2)}) copy-start(bf16[1024,256]{1,0:T(8,128)(2,1)} %up_own.3) | copy-start | bytes 1572868
  27.3 16.8 %copy-start.4 = (bf16[256,1024]{1,0:T(8,128)(2,1)S(1)}, bf16[256,1024]{1,0:T(8,128)(2,1)}, u32[]{:S(2)}) copy-start(bf16[256,1024]{1,0:T(8,128)(2,1)} %down_own.1) | copy-start | bytes 1572868
  27.4 16.8 %copy-start.6 = (bf16[256,1024]{1,0:T(8,128)(2,1)S(1)}, bf16[256,1024]{1,0:T(8,128)(2,1)}, u32[]{:S(2)}) copy-start(bf16[256,1024]{1,0:T(8,128)(2,1)} %copy-done.5) | copy-start | bytes 1572868
  46.2 13.0 %all-to-all-start.2 = ((s16[4,784,128]{2,1,0:T(8,128)(2,1)}), s16[4,784,128]{2,1,0:T(8,128)(2,1)S(1)}, u32[]{:S(2)}, u32[]{:S(2)}) async-start(s16[4,784,128]{2,1,0:T(8,128)(2,1)} %shard_map.120), calls=%async_computation.2 | async-start | bytes 1605632 | tf_op jit(solution)/shard_map/all_to_all | solution.py:214
  51.1 50.5 %collective-permute-start.4 = (bf16[256,2048]{1,0:T(8,128)(2,1)S(1)}, bf16[256,2048]{1,0:T(8,128)(2,1)}, u32[]{:S(2)}, u32[]{:S(2)}) collective-permute-start(bf16[256,2048]{1,0:T(8,128)(2,1)S(1)} %bitcast.12), channel_id=1, source_target_pairs={{0,1},{1,0},{2,3},{3,2},{4,5},{5,4},{6,7},{7,6},{8,9},{9,8},{10,11... | collective-permute-start | bytes 3145736 | tf_op jit(solution)/shard_map/ppermute | solution.py:206
  75.0 13.4 %copy-start.3 = (bf16[1024,256]{1,0:T(8,128)(2,1)S(1)}, bf16[1024,256]{1,0:T(8,128)(2,1)}, u32[]{:S(2)}) copy-start(bf16[1024,256]{1,0:T(8,128)(2,1)} %copy-done.2) | copy-start | bytes 1572868
  89.9 3.6 %copy-start.11 = (bf16[256,768]{1,0:T(8,128)(2,1)S(1)}, bf16[256,768]{1,0:T(8,128)(2,1)}, u32[]{:S(2)}) copy-start(bf16[256,768]{1,0:T(8,128)(2,1)} %get-tuple-element.21) | copy-start | bytes 1179652
  89.9 11.7 %all-to-all-start.3 = ((bf16[4,64,1024]{2,1,0:T(8,128)(2,1)}), bf16[4,64,1024]{2,1,0:T(8,128)(2,1)S(1)}, u32[]{:S(2)}, u32[]{:S(2)}) async-start(bf16[4,64,1024]{2,1,0:T(8,128)(2,1)} %get-tuple-element.20), calls=%async_computation.3 | async-start | bytes 1048576 | tf_op jit(solution)/shard_map/all_to_all | solution.py:224
  93.5 8.0 %collective-permute-start.3 = (bf16[256,768]{1,0:T(8,128)(2,1)S(1)}, bf16[256,768]{1,0:T(8,128)(2,1)S(1)}, u32[]{:S(2)}, u32[]{:S(2)}) collective-permute-start(bf16[256,768]{1,0:T(8,128)(2,1)S(1)} %copy-done.11), channel_id=1, source_target_pairs={{0,1},{1,0},{2,3},{3,2},{4,5},{5,4},{6,7},{7,6},{8,9},{9,8},{10,11... | collective-permute-start | bytes 1179656 | tf_op jit(solution)/shard_map/ppermute | solution.py:206
  102.3 15.9 %copy-start.10 = (s32[1,1,3]{2,1,0:T(1,128)S(1)}, s32[1,1,3]{2,1,0:T(1,128)}, u32[]{:S(2)}) copy-start(s32[1,1,3]{2,1,0:T(1,128)} %param.17) | copy-start | bytes 40
  102.3 22.7 %all-to-all-start.4 = ((bf16[8,8,1024]{2,1,0:T(8,128)(2,1)}), bf16[8,8,1024]{2,1,0:T(8,128)(2,1)S(1)}, u32[]{:S(2)}, u32[]{:S(2)}) async-start(bf16[8,8,1024]{2,1,0:T(8,128)(2,1)} %bitcast.4), calls=%async_computation.4 | async-start | bytes 262144 | tf_op jit(solution)/shard_map/all_to_all | solution.py:228
  118.2 0.7 copy-start.7
  118.2 0.7 copy-start.8
  118.2 0.7 copy-start.9
